TPU v7x, 32 devices: a whole 2x2x4 slice. The times are simulated.
32 devices in a mesh: group: 2 (over y), tile: 4 (over z), view: 2 (over x), sub: 2 (over core).
Axes of the slice: x: 2, y: 2, z: 4, core: 2. Of those that a mesh axis runs over, the one named last changes fastest.
Arguments:
- centers: float32 [3, 131072], P(None, ('group', 'tile', 'view', 'sub')), parts along dimension 1, may hold values from -2 to 2
- scale_log: float32 [3, 131072], P(None, ('group', 'tile', 'view', 'sub')), parts along dimension 1, may hold values from -6.2 to -3.9
- shear_terms: float32 [3, 131072], P(None, ('group', 'tile', 'view', 'sub')), parts along dimension 1, may hold values from -3 to 3
- opacity_logit: float32 [131072], P(('group', 'tile', 'view', 'sub')), parts along dimension 0, may hold values from -7 to -2
- sh_coeffs: float32 [48, 131072], P(None, ('group', 'tile', 'view', 'sub')), parts along dimension 1, may hold values from -3 to 3
- cameras: float32 [4, 8], P('group'), parts along dimension 0, may hold values from -100 to 600, as said below
- appearance: float32 [4, 12], P(('group', 'view')), parts along dimension 0, may hold values from -1 to 1
- target: float32 [3, 4, 8, 8, 256], P(None, ('group', 'view'), ('tile', 'sub')), parts along dimension 1, may hold values from 0 to 1
- send_index: int32 [32, 16, 256], P(('group', 'tile', 'view', 'sub')), parts along dimension 0, may hold values from 0 to 4095, as said below
- send_count: int32 [32, 16], P(('group', 'tile', 'view', 'sub')), parts along dimension 0, may hold values from 1 to 256, as said below
- tile_list: int32 [32, 8, 512], P(('group', 'tile', 'view', 'sub')), parts along dimension 0, may hold values from 0 to 4095, as said below
- tile_count: int32 [32, 8], P(('group', 'tile', 'view', 'sub')), parts along dimension 0, may hold values from 1 to 512
Outputs:
- rendered: float32 [3, 4, 8, 8, 256], P(None, ('group', 'view'), ('tile', 'sub')), parts along dimension 1
- param_grad: float32 [58, 131072], P(None, ('group', 'tile', 'view', 'sub')), parts along dimension 1
- appearance_grad: float32 [4, 12], P(('group', 'view')), parts along dimension 0
There are 2 independent parts, one for each index of `group`. A program takes and returns all parts, laid end to end along the dimension named above; each array names one. Nothing has to cross between parts.
Inputs may be any that keep to these rules, and one draw needn't show every extreme that they name: `send_index`: the 16 x 256 slots of device s name each of its Gaussians once, so a Gaussian is sent to at most one device; slots j >= send_count[s, d] are unused. `send_count`: some device receives 256 rows from every device. `tile_list`: live entries index the device's pool; every pool item stands in exactly one list; empty entries are 0. `cameras`: columns fx, sx, cx, fy, sy, cy, polar, azimuth; fx and fy lie in 300 to 600.
All inputs are finite; a program needn't handle non-finite values.
Results may differ from a plain program's by a relative error of at most 0.0003.
Values sent between devices are 32-bit elements; how exact they have to be, the bound alone decides.
A program may use at most 128 MiB of HBM per device.

v0:
```python
import functools

import jax
import jax.numpy as jnp
from jax import lax
from jax.experimental import pallas as pl
from jax.experimental.pallas import tpu as pltpu
from jax.sharding import PartitionSpec as P

F32 = jnp.float32
BF16 = jnp.bfloat16
I32 = jnp.int32
LOG2E = 1.4426950408889634
LANES = 128
ROUTE_AXES = ("tile", "view", "sub")
NT = (((1,), (1,)), ((), ()))
PARAMS = pltpu.CompilerParams(vmem_limit_bytes=48 * 1024 * 1024)
IN_VMEM = pl.BlockSpec(memory_space=pltpu.VMEM)
IN_SMEM = pl.BlockSpec(memory_space=pltpu.SMEM)


def harmonic_table(cameras):
    polar_angle = cameras[:, 6]
    azimuth = cameras[:, 7]
    unit_x = jnp.sin(polar_angle) * jnp.cos(azimuth)
    unit_y = jnp.sin(polar_angle) * jnp.sin(azimuth)
    unit_z = jnp.cos(polar_angle)
    square_x = unit_x * unit_x
    square_y = unit_y * unit_y
    square_z = unit_z * unit_z
    columns = [
        jnp.full_like(unit_x, 0.28209479177387814),
        -0.4886025119029199 * unit_y,
        0.4886025119029199 * unit_z,
        -0.4886025119029199 * unit_x,
        1.0925484305920792 * unit_x * unit_y,
        -1.0925484305920792 * unit_y * unit_z,
        0.31539156525252005 * (2.0 * square_z - square_x - square_y),
        -1.0925484305920792 * unit_x * unit_z,
        0.5462742152960396 * (square_x - square_y),
        -0.5900435899266435 * unit_y * (3.0 * square_x - square_y),
        2.890611442640554 * unit_x * unit_y * unit_z,
        -0.4570457994644658 * unit_y * (4.0 * square_z - square_x - square_y),
        0.3731763325901154 * unit_z * (2.0 * square_z - 3.0 * square_x - 3.0 * square_y),
        -0.4570457994644658 * unit_x * (4.0 * square_z - square_x - square_y),
        1.445305721320277 * unit_z * (square_x - square_y),
        -0.5900435899266435 * unit_x * (square_x - 3.0 * square_y),
    ]
    return jnp.stack(columns, axis=0)


def project_shape(p0, p1, p2, p3, p4, p5, p6, p7, p8, camera):
    focal_x, skew_x, center_x, focal_y, skew_y, center_y = camera
    mean_x = focal_x * p0 + skew_x * p2 + center_x
    mean_y = focal_y * p1 + skew_y * p2 + center_y
    factor_xx = jnp.exp(p3)
    factor_yy = jnp.exp(p4)
    factor_zz = jnp.exp(p5)
    factor_yx = p6 * factor_xx
    factor_zx = p7 * factor_xx
    factor_zy = p8 * factor_yy
    upper_x = focal_x * factor_xx + skew_x * factor_zx
    upper_y = skew_x * factor_zy
    upper_z = skew_x * factor_zz
    below_x = focal_y * factor_yx + skew_y * factor_zx
    below_y = focal_y * factor_yy + skew_y * factor_zy
    below_z = skew_y * factor_zz
    spread_xx = upper_x * upper_x + upper_y * upper_y + upper_z * upper_z + 0.3
    spread_xy = upper_x * below_x + upper_y * below_y + upper_z * below_z
    spread_yy = below_x * below_x + below_y * below_y + below_z * below_z + 0.3
    inverse = 1.0 / (spread_xx * spread_yy - spread_xy * spread_xy)
    return (mean_x, mean_y, spread_yy * inverse, -spread_xy * inverse, spread_xx * inverse)


def lane_gather(values, lanes):
    dims = lax.GatherDimensionNumbers(
        offset_dims=(),
        collapsed_slice_dims=(1,),
        start_index_map=(1,),
        operand_batching_dims=(0,),
        start_indices_batching_dims=(0,),
    )
    return lax.gather(
        values,
        lanes[:, :, None],
        dims,
        slice_sizes=(1, 1),
        mode=lax.GatherScatterMode.PROMISE_IN_BOUNDS,
    )


def spread(row, rows):
    return jnp.broadcast_to(row, (rows, row.shape[1]))


def iota(shape, dim):
    return lax.broadcasted_iota(I32, shape, dim)


def onehot_scatter(total, high, low, first, second, live):
    blocks = total.shape[0] // 2
    hit = iota((blocks, LANES), 0) == high
    if live is not None:
        hit = jnp.logical_and(hit, live)
    left = jnp.concatenate(
        [jnp.where(hit, first, 0.0), jnp.where(hit, second, 0.0)], axis=0
    ).astype(BF16)
    right = (iota((LANES, LANES), 0) == low).astype(F32).astype(BF16)
    return total + lax.dot_general(left, right, NT, preferred_element_type=F32)


def gather_columns(out_ref, source_ref, high_ref, low_ref):
    out_blocks = high_ref.shape[0]
    blocks = source_ref.shape[1] // LANES

    def one_block(place, carry):
        high = spread(high_ref[pl.ds(place, 1), :], 8)
        low = spread(low_ref[pl.ds(place, 1), :], 8)
        found = jnp.zeros((8, LANES), F32)
        for block in range(blocks):
            cut = slice(block * LANES, (block + 1) * LANES)
            found = jnp.where(high == block, lane_gather(source_ref[0:8, cut], low), found)
        out_ref[0:8, pl.ds(pl.multiple_of(place * LANES, LANES), LANES)] = found
        return carry

    lax.fori_loop(0, out_blocks, one_block, 0)
    for group in range(out_blocks // 8):
        high = high_ref[group * 8 : group * 8 + 8, :]
        low = low_ref[group * 8 : group * 8 + 8, :]
        found = jnp.zeros((8, LANES), F32)
        for block in range(blocks):
            cut = slice(block * LANES, (block + 1) * LANES)
            row = spread(source_ref[8:9, cut], 8)
            found = jnp.where(high == block, lane_gather(row, low), found)
        for inner in range(8):
            place = group * 8 + inner
            out_ref[8:9, place * LANES : (place + 1) * LANES] = found[inner : inner + 1, :]


def select_camera(cameras_ref, view):
    chosen = []
    for column in range(6):
        value = jnp.full(view.shape, cameras_ref[0, column], F32)
        for other in range(1, cameras_ref.shape[0]):
            value = jnp.where(view == other, cameras_ref[other, column], value)
        chosen.append(value)
    return chosen


def select_harmonics(harmonics_ref, view):
    shape = (16, view.shape[1])
    value = jnp.broadcast_to(harmonics_ref[:, 0:1], shape)
    for other in range(1, harmonics_ref.shape[1]):
        value = jnp.where(
            view == other, jnp.broadcast_to(harmonics_ref[:, other : other + 1], shape), value
        )
    return value


def owner_kernel(
    sub_count,
    view_count,
    slot_cap,
    centers_ref,
    scale_ref,
    shear_ref,
    opacity_ref,
    coeff_ref,
    cameras_ref,
    harmonics_ref,
    slots_ref,
    count_ref,
    out_ref,
    place_ref,
    owner_ref,
    high_ref,
    low_ref,
    projected_ref,
):
    blocks = slots_ref.shape[0]
    slots = slots_ref[...]
    high_ref[...] = slots >> 7
    low_ref[...] = slots & 127
    peers = count_ref.shape[1]

    lane = iota((blocks, LANES), 1)

    def one_block(place, total):
        return onehot_scatter(
            total,
            high_ref[pl.ds(place, 1), :],
            low_ref[pl.ds(place, 1), :],
            place.astype(F32),
            lane.astype(F32),
            None,
        )

    table = lax.fori_loop(0, blocks, one_block, jnp.zeros((2 * blocks, LANES), F32)).astype(I32)
    place_ref[...] = table
    position = table[0:blocks] * LANES + table[blocks:]
    dest = position // slot_cap
    view = (dest // sub_count) % view_count
    within = position - dest * slot_cap
    limit = jnp.zeros_like(dest)
    for peer in range(peers):
        limit = jnp.where(dest == peer, count_ref[0, peer], limit)
    live = (within < limit).astype(I32)
    for block in range(blocks):
        cut = slice(block * LANES, (block + 1) * LANES)
        owner_ref[0:1, cut] = view[block : block + 1, :]
        owner_ref[1:2, cut] = live[block : block + 1, :]

    step = 512

    def one_chunk(number, carry):
        cut = pl.ds(pl.multiple_of(number * step, step), step)
        view_row = owner_ref[0:1, cut]
        camera = select_camera(cameras_ref, view_row)
        params = [ref[r : r + 1, cut] for ref in (centers_ref, scale_ref, shear_ref) for r in range(3)]
        rows = list(project_shape(*params, camera))
        logit = opacity_ref[0:1, cut]
        rows.append(jnp.minimum(logit, 0.0) - jnp.log1p(jnp.exp(-jnp.abs(logit))))
        basis = select_harmonics(harmonics_ref, view_row)
        for color in range(3):
            terms = coeff_ref[color * 16 : color * 16 + 16, cut] * basis
            rows.append(jnp.maximum(jnp.sum(terms, axis=0, keepdims=True) + 0.5, 0.0))
        for row in range(9):
            projected_ref[row : row + 1, cut] = rows[row]
        return carry

    lax.fori_loop(0, coeff_ref.shape[1] // step, one_chunk, 0)
    out_ref[8:16, :] = jnp.zeros((8, out_ref.shape[1]), F32)
    gather_columns(out_ref, projected_ref, high_ref, low_ref)
    for peer in range(peers):
        out_ref[9:10, peer * slot_cap : (peer + 1) * slot_cap] = jnp.full(
            (1, slot_cap), count_ref[0, peer].astype(F32)
        )


def tile_kernel(
    slot_cap,
    peers,
    sub_count,
    pool_ref,
    list_ref,
    count_ref,
    appear_ref,
    target_ref,
    out_ref,
    rendered_ref,
    entry_ref,
    alpha_ref,
    weight_ref,
    moment_ref,
    gathered_ref,
    high_ref,
    low_ref,
):
    tiles, list_len = list_ref.shape
    tile_pix = target_ref.shape[2]
    blocks = pool_ref.shape[1] // LANES
    cols = list_len // LANES
    halves = tile_pix // LANES
    tile_row = lax.axis_index("tile") * sub_count + lax.axis_index("sub")
    center_y = 16.0 * tile_row.astype(F32) + 7.5

    entries = list_ref[...]
    column = entries
    inclusive = jnp.zeros((1, LANES), I32)
    for peer in range(peers):
        start = peer * slot_cap
        received = jnp.broadcast_to(pool_ref[9:10, start : start + 1], (1, LANES)).astype(I32)
        inclusive = inclusive + received
        bound = jnp.concatenate([spread(inclusive, tiles)] * cols, axis=1)
        gap = jnp.concatenate([spread(slot_cap - received, tiles)] * cols, axis=1)
        column = column + jnp.where(bound <= entries, gap, 0)
    column = jnp.clip(column, 0, pool_ref.shape[1] - 1)
    lane = iota((tiles, list_len), 1)
    tile = iota((tiles, list_len), 0)
    live_limit = jnp.zeros((tiles, list_len), I32)
    for number in range(tiles):
        live_limit = jnp.where(tile == number, count_ref[0, number], live_limit)
    live = lane < live_limit
    high_all = column >> 7
    low_all = column & 127

    tile_x = 16.0 * iota((tiles, LANES), 0).astype(F32) + 7.5
    for col in range(cols):
        cut = slice(col * LANES, (col + 1) * LANES)
        high = high_all[:, cut]
        low = low_all[:, cut]
        found = [jnp.zeros((tiles, LANES), F32) for _ in range(9)]
        for block in range(blocks):
            hit = high == block
            for row in range(9):
                source = spread(pool_ref[row : row + 1, block * LANES : (block + 1) * LANES], tiles)
                found[row] = jnp.where(hit, lane_gather(source, low), found[row])
        found[0] = found[0] - tile_x
        found[1] = found[1] - center_y
        found[2] = found[2] * (-0.5 * LOG2E)
        found[3] = found[3] * (-LOG2E)
        found[4] = found[4] * (-0.5 * LOG2E)
        found[5] = jnp.where(live[:, cut], found[5] * LOG2E, -1e30)
        for row in range(9):
            entry_ref[row * cols + col] = found[row]

    pixel = iota((tiles, LANES), 1)
    pixel_x = (pixel & 15).astype(F32) - 7.5
    pixel_y = [((pixel + half * LANES) >> 4).astype(F32) - 7.5 for half in range(halves)]

    state = (
        tuple(jnp.ones((tiles, LANES), F32) for _ in range(halves)),
        tuple(jnp.zeros((tiles, LANES), F32) for _ in range(3 * halves)),
    )
    for col in range(cols):

        def forward(k, state, col=col):
            transmit, colors = state
            at = jnp.full((tiles, LANES), k, I32)
            row = [lane_gather(entry_ref[r * cols + col], at) for r in range(9)]
            delta_x = row[0] - pixel_x
            part = row[2] * delta_x * delta_x + row[5]
            slope = row[3] * delta_x
            new_transmit = []
            new_colors = []
            for half in range(halves):
                delta_y = row[1] - pixel_y[half]
                alpha = jnp.exp2(part + delta_y * (slope + row[4] * delta_y))
                weight = alpha * transmit[half]
                cut = slice(half * LANES, (half + 1) * LANES)
                alpha_ref[col * LANES + k, :, cut] = alpha
                weight_ref[col * LANES + k, :, cut] = weight
                new_transmit.append(transmit[half] * (1.0 - alpha))
                for color in range(3):
                    new_colors.append(colors[half * 3 + color] + weight * row[6 + color])
            return (tuple(new_transmit), tuple(new_colors))

        state = lax.fori_loop(0, LANES, forward, state, unroll=8)
    blended = [
        jnp.concatenate([state[1][half * 3 + color] for half in range(halves)], axis=1)
        for color in range(3)
    ]

    mixing = [
        [appear_ref[0, 3 * c + d] + (1.0 if c == d else 0.0) for d in range(3)] for c in range(3)
    ]
    residue = []
    for c in range(3):
        value = appear_ref[0, 9 + c]
        value = (
            mixing[c][0] * blended[0] + mixing[c][1] * blended[1] + mixing[c][2] * blended[2] + value
        )
        rendered_ref[c] = value
        residue.append(value - target_ref[c])
    back = [
        mixing[0][d] * residue[0] + mixing[1][d] * residue[1] + mixing[2][d] * residue[2]
        for d in range(3)
    ]
    sums = [residue[c] * blended[d] for c in range(3) for d in range(3)] + residue
    term_lane = iota((1, slot_cap), 1)
    term_row = jnp.zeros((1, slot_cap), F32)
    for number, values in enumerate(sums):
        total = jnp.sum(jnp.sum(values, axis=0, keepdims=True), axis=1, keepdims=True)
        term_row = jnp.where(term_lane == number, total, term_row)

    back_half = [
        [back[c][:, half * LANES : (half + 1) * LANES] for c in range(3)] for half in range(halves)
    ]
    behind = tuple(jnp.zeros((tiles, LANES), F32) for _ in range(halves))
    for col in reversed(range(cols)):

        def backward(number, behind, col=col):
            k = LANES - 1 - number
            at = jnp.full((tiles, LANES), k, I32)
            row = [lane_gather(entry_ref[r * cols + col], at) for r in (6, 7, 8)]
            new_behind = []
            for half in range(halves):
                cut = slice(half * LANES, (half + 1) * LANES)
                seen = (
                    back_half[half][0] * row[0]
                    + back_half[half][1] * row[1]
                    + back_half[half][2] * row[2]
                )
                ahead = seen - behind[half]
                alpha = alpha_ref[col * LANES + k, :, cut]
                new_behind.append(behind[half] + alpha * ahead)
                alpha_ref[col * LANES + k, :, cut] = ahead * weight_ref[col * LANES + k, :, cut]
            return tuple(new_behind)

        behind = lax.fori_loop(0, LANES, backward, behind, unroll=8)

    pix = iota((16, tile_pix), 1)
    mono_x = (pix & 15).astype(F32) - 7.5
    mono_y = (pix >> 4).astype(F32) - 7.5
    kind = iota((16, tile_pix), 0)
    mono = jnp.where(kind == 0, 1.0, 0.0)
    for number, values in enumerate(
        (mono_x, mono_y, mono_x * mono_x, mono_x * mono_y, mono_y * mono_y)
    ):
        mono = jnp.where(kind == number + 1, values, mono)
    mono = mono.astype(BF16)
    back_all = jnp.concatenate(back, axis=0)
    back_high = back_all.astype(BF16)
    back_low = (back_all - back_high.astype(F32)).astype(BF16)
    back_both = jnp.concatenate([back_high, back_low], axis=0)
    steps = 32
    width = steps * tiles
    own_tile = iota((tiles, width), 0) == (iota((tiles, width), 1) & (tiles - 1))

    def reduce_pixels(number, carry):
        cut = pl.ds(pl.multiple_of(number * width, width), width)
        power = alpha_ref[pl.ds(number * steps, steps)].reshape(width, tile_pix)
        power_high = power.astype(BF16)
        power_low = (power - power_high.astype(F32)).astype(BF16)
        moments = lax.dot_general(mono, power_high, NT, preferred_element_type=F32)
        moments = moments + lax.dot_general(mono, power_low, NT, preferred_element_type=F32)
        moment_ref[0:8, cut] = moments[0:8]
        weight = weight_ref[pl.ds(number * steps, steps)].reshape(width, tile_pix)
        weight_high = weight.astype(BF16)
        weight_low = (weight - weight_high.astype(F32)).astype(BF16)
        colors = lax.dot_general(back_both, weight_high, NT, preferred_element_type=F32)
        colors = colors[: 3 * tiles] + colors[3 * tiles :]
        colors = colors + lax.dot_general(back_high, weight_low, NT, preferred_element_type=F32)
        for color in range(3):
            own = jnp.where(own_tile, colors[color * tiles : (color + 1) * tiles], 0.0)
            moment_ref[6 + color : 7 + color, cut] = jnp.sum(own, axis=0, keepdims=True)
        return carry

    lax.fori_loop(0, list_len // steps, reduce_pixels, 0)

    table = jnp.zeros((2 * blocks, LANES), F32)
    place_lane = iota((1, LANES), 1)
    for number in range(tiles):
        for col in range(cols):
            cut = slice(col * LANES, (col + 1) * LANES)
            k = place_lane + col * LANES
            flat = k * tiles + number
            table = onehot_scatter(
                table,
                high_all[number : number + 1, cut],
                low_all[number : number + 1, cut],
                (flat >> 7).astype(F32),
                (flat & 127).astype(F32),
                k < count_ref[0, number],
            )
    table = table.astype(I32)
    high_ref[...] = table[0:blocks]
    low_ref[...] = table[blocks:]
    gather_columns(gathered_ref, moment_ref, high_ref, low_ref)

    for block in range(blocks):
        cut = slice(block * LANES, (block + 1) * LANES)
        own = (table[blocks + block : blocks + block + 1, :] & (tiles - 1)).astype(F32)
        local_x = pool_ref[0:1, cut] - (16.0 * own + 7.5)
        local_y = pool_ref[1:2, cut] - center_y
        conic_a = pool_ref[2:3, cut]
        conic_b = pool_ref[3:4, cut]
        conic_c = pool_ref[4:5, cut]
        one, m_x, m_y, m_xx, m_xy, m_yy = [gathered_ref[r : r + 1, cut] for r in range(6)]
        d_x = local_x * one - m_x
        d_y = local_y * one - m_y
        d_xx = local_x * d_x - (local_x * m_x - m_xx)
        d_xy = local_y * d_x - (local_x * m_y - m_xy)
        d_yy = local_y * d_y - (local_y * m_y - m_yy)
        out_ref[0:1, cut] = -(conic_a * d_x + conic_b * d_y)
        out_ref[1:2, cut] = -(conic_c * d_y + conic_b * d_x)
        out_ref[2:3, cut] = -0.5 * d_xx
        out_ref[3:4, cut] = -d_xy
        out_ref[4:5, cut] = -0.5 * d_yy
        out_ref[5:6, cut] = one
    out_ref[6:8, :] = gathered_ref[6:8, :]
    out_ref[8:16, :] = jnp.zeros((8, out_ref.shape[1]), F32)
    out_ref[8:9, :] = gathered_ref[8:9, :]
    for peer in range(peers):
        out_ref[9:10, peer * slot_cap : (peer + 1) * slot_cap] = term_row


def gradient_kernel(
    sub_count,
    view_count,
    slot_cap,
    peers,
    pixels,
    centers_ref,
    scale_ref,
    shear_ref,
    opacity_ref,
    coeff_ref,
    cameras_ref,
    harmonics_ref,
    place_ref,
    owner_ref,
    back_ref,
    out_ref,
    appear_ref,
    gathered_ref,
    high_ref,
    low_ref,
):
    blocks = high_ref.shape[0]
    high_ref[...] = place_ref[0:blocks, :]
    low_ref[...] = place_ref[blocks:, :]
    gather_columns(gathered_ref, back_ref, high_ref, low_ref)
    step = 512

    def one_chunk(number, carry):
        cut = pl.ds(pl.multiple_of(number * step, step), step)
        view_row = owner_ref[0:1, cut]
        live = owner_ref[1:2, cut] > 0
        grads = [jnp.where(live, gathered_ref[r : r + 1, cut], 0.0) for r in range(9)]
        camera = select_camera(cameras_ref, view_row)
        params = [ref[r : r + 1, cut] for ref in (centers_ref, scale_ref, shear_ref) for r in range(3)]
        _, pullback = jax.vjp(lambda *rows: project_shape(*rows, camera), *params)
        for row, value in enumerate(pullback(tuple(grads[:5]))):
            out_ref[row : row + 1, cut] = value
        out_ref[9:10, cut] = grads[5] / (1.0 + jnp.exp(opacity_ref[0:1, cut]))
        basis = select_harmonics(harmonics_ref, view_row)
        for color in range(3):
            terms = coeff_ref[color * 16 : color * 16 + 16, cut] * basis
            value = jnp.sum(terms, axis=0, keepdims=True) + 0.5
            slope = jnp.where(value > 0.0, 1.0, jnp.where(value == 0.0, 0.5, 0.0))
            out_ref[10 + 16 * color : 26 + 16 * color, cut] = basis * (slope * grads[6 + color])
        return carry

    lax.fori_loop(0, coeff_ref.shape[1] // step, one_chunk, 0)
    mine = lax.axis_index("view")
    total = jnp.zeros((1, slot_cap), F32)
    for peer in range(peers):
        same = ((peer // sub_count) % view_count == mine).astype(F32)
        total = total + same * back_ref[9:10, peer * slot_cap : (peer + 1) * slot_cap]
    appear_ref[...] = (total * (1.0 / pixels))[:, :12]


def exchange(rows):
    return lax.all_to_all(rows, ROUTE_AXES, split_axis=1, concat_axis=1, tiled=True)


def on_device(
    centers,
    scale_log,
    shear_terms,
    opacity_logit,
    sh_coeffs,
    cameras,
    appearance,
    target,
    send_index,
    send_count,
    tile_list,
    tile_count,
):
    peers, slot_cap = send_index.shape[1:]
    slots = peers * slot_cap
    blocks = slots // LANES
    gauss_count = centers.shape[1]
    tiles, list_len = tile_list.shape[1:]
    tile_pix = target.shape[-1]
    sub_count = lax.axis_size("sub")
    view_count = lax.axis_size("view")
    tile_devs = lax.axis_size("tile")
    harmonics = harmonic_table(cameras)
    opacity_row = opacity_logit[None, :]
    source = (centers, scale_log, shear_terms, opacity_row, sh_coeffs, cameras, harmonics)
    source_specs = [IN_VMEM] * 5 + [IN_SMEM, IN_VMEM]
    outgoing, place, owner = pl.pallas_call(
        functools.partial(owner_kernel, sub_count, view_count, slot_cap),
        out_shape=(
            jax.ShapeDtypeStruct((16, slots), F32),
            jax.ShapeDtypeStruct((2 * blocks, LANES), I32),
            jax.ShapeDtypeStruct((8, gauss_count), I32),
        ),
        in_specs=source_specs + [IN_VMEM, IN_SMEM],
        out_specs=(IN_VMEM,) * 3,
        scratch_shapes=[
            pltpu.VMEM((blocks, LANES), I32),
            pltpu.VMEM((blocks, LANES), I32),
            pltpu.VMEM((16, gauss_count), F32),
        ],
        compiler_params=PARAMS,
        name="owner_rows",
    )(*source, send_index.reshape(blocks, LANES), send_count)
    arrived = exchange(outgoing)
    returning, rendered = pl.pallas_call(
        functools.partial(tile_kernel, slot_cap, peers, sub_count),
        out_shape=(
            jax.ShapeDtypeStruct((16, slots), F32),
            jax.ShapeDtypeStruct((3, tiles, tile_pix), F32),
        ),
        in_specs=[IN_VMEM, IN_VMEM, IN_SMEM, IN_SMEM, IN_VMEM],
        out_specs=(IN_VMEM,) * 2,
        scratch_shapes=[
            pltpu.VMEM((9 * list_len // LANES, tiles, LANES), F32),
            pltpu.VMEM((list_len, tiles, tile_pix), F32),
            pltpu.VMEM((list_len, tiles, tile_pix), F32),
            pltpu.VMEM((16, tiles * list_len), F32),
            pltpu.VMEM((16, slots), F32),
            pltpu.VMEM((blocks, LANES), I32),
            pltpu.VMEM((blocks, LANES), I32),
        ],
        compiler_params=PARAMS,
        name="tile_blend",
    )(arrived, tile_list[0], tile_count, appearance, target[:, 0, 0])
    returned = exchange(returning)
    param_grad, appearance_grad = pl.pallas_call(
        functools.partial(
            gradient_kernel,
            sub_count,
            view_count,
            slot_cap,
            peers,
            float(tile_devs * sub_count * tiles * tile_pix),
        ),
        out_shape=(
            jax.ShapeDtypeStruct((10 + sh_coeffs.shape[0], gauss_count), F32),
            jax.ShapeDtypeStruct((1, 12), F32),
        ),
        in_specs=source_specs + [IN_VMEM] * 3,
        out_specs=(IN_VMEM,) * 2,
        scratch_shapes=[
            pltpu.VMEM((16, gauss_count), F32),
            pltpu.VMEM((blocks, LANES), I32),
            pltpu.VMEM((blocks, LANES), I32),
        ],
        compiler_params=PARAMS,
        name="owner_gradient",
    )(*source, place, owner, returned)
    return (rendered[:, None, None], param_grad, appearance_grad)


def solution(mesh):
    return jax.shard_map(
        on_device,
        mesh=mesh,
        in_specs=(
            P(None, ("group", "tile", "view", "sub")),
            P(None, ("group", "tile", "view", "sub")),
            P(None, ("group", "tile", "view", "sub")),
            P(("group", "tile", "view", "sub")),
            P(None, ("group", "tile", "view", "sub")),
            P("group", None),
            P(("group", "view"), None),
            P(None, ("group", "view"), ("tile", "sub"), None, None),
            P(("group", "tile", "view", "sub"), None, None),
            P(("group", "tile", "view", "sub"), None),
            P(("group", "tile", "view", "sub"), None, None),
            P(("group", "tile", "view", "sub"), None),
        ),
        out_specs=(
            P(None, ("group", "view"), ("tile", "sub"), None, None),
            P(None, ("group", "tile", "view", "sub")),
            P(("group", "view"), None),
        ),
        check_vma=False,
    )
```

profile of v0, /device:TPU:0, one launch (start us, length us, event | category | flops | bytes accessed | tf_op | source)
XLA Modules:
  0.0 84.5 jit_solution(10133083242538780618)
XLA Ops:
  0.6 0.0 copy-start.8
  0.6 0.9 %sine_multiply_fusion = (f32[2,1]{1,0:T(2,128)S(1)}, f32[2,1]{1,0:T(2,128)S(1)}) fusion(f32[2,8]{1,0:T(2,128)} %cameras_ref.3), kind=kLoop, calls=%fused_computation.20 | loop fusion | flops 4 | bytes 32 | tf_op jit(solution)/shard_map/mul | solution.py:26
  1.5 0.0 copy-start.2
  1.6 0.0 copy-start.3
  1.6 0.8 reshape.369.slots_ref
  2.3 0.0 copy-done.8
  2.3 0.4 multiply_reduce_fusion.8
  2.8 0.1 stack.2.harmonics_ref
  2.9 0.0 copy-start.11
  2.9 0.0 copy-done.2
  2.9 0.0 copy-done.3
  2.9 0.6 copy-done.11
  3.5 0.0 copy-start
  3.5 1.1 %copy-done = f32[48,4096]{1,0:T(8,128)S(1)} copy-done((f32[48,4096]{1,0:T(8,128)S(1)}, f32[48,4096]{1,0:T(8,128)}, u32[]{:S(2)}) %copy-start) | copy-done | bytes 786456
  4.6 0.0 copy-start.4
  4.6 0.8 copy-done.4
  5.5 0.0 copy-start.6
  5.5 0.7 copy-done.6
  6.2 9.9 %owner_rows.1 = (f32[16,4096]{1,0:T(8,128)S(1)}, s32[64,128]{1,0:T(8,128)S(1)}, s32[8,4096]{1,0:T(8,128)S(1)}) custom-call(f32[3,4096]{1,0:T(4,128)S(1)} %copy-done.2, f32[3,4096]{1,0:T(4,128)S(1)} %copy-done.3, f32[3,4096]{1,0:T(4,128)S(1)} %copy-done.4, f32[1,4096]{1,0:T(1,128)S(1)} %bitcast.91, f32[48,4096]{1,0:T(8,128)S(1)} %copy-done, ...), custom_call_target="tpu_custom_call" | custom-call | tf_op jit(solution)/shard_map/owner_rows/pallas_call | solution.py:565
  16.1 17.2 %all_to_all.22 = f32[16,16,256]{2,0,1:T(8,128)S(1)} all-to-all(f32[16,16,256]{2,0,1:T(8,128)S(1)} %bitcast.95), channel_id=1, replica_groups=mesh['group'=2,'tile'=4,'view'=2,'sub'=2] {'tile','view','sub'}, dimensions={1} | all-to-all | bytes 524288 | tf_op jit(solution)/shard_map/all_to_all | solution.py:535
  33.3 0.0 copy-start.9
  33.3 0.0 copy-start.10
  33.3 0.0 copy-start.12
  33.3 0.0 copy-start.13
  33.3 0.7 copy-done.9
  34.0 0.0 copy-done.10
  34.0 0.0 copy-done.12
  34.0 0.0 copy-done.13
  34.0 30.7 %tile_blend.1 = (f32[16,4096]{1,0:T(8,128)S(1)}, f32[3,8,256]{2,1,0:T(8,128)}) custom-call(f32[16,4096]{1,0:T(8,128)S(1)} %bitcast.88, s32[8,512]{1,0:T(8,128)S(1)} %bitcast.94, s32[1,8]{1,0:T(1,128)S(1)} %copy-done.12, f32[1,12]{1,0:T(1,128)S(1)} %copy-done.13, f32[3,8,256]{2,1,0:T(8,128)S(1)} %bitcast.93), custom_call_target="tpu_custom_call" | custom-call | tf_op jit(solution)/shard_map/tile_blend/pallas_call | solution.py:583
  64.7 0.0 copy-start.1
  64.7 13.0 %all_to_all.23 = f32[16,16,256]{2,0,1:T(8,128)S(1)} all-to-all(f32[16,16,256]{2,0,1:T(8,128)S(1)} %bitcast.97), channel_id=1, replica_groups=mesh['group'=2,'tile'=4,'view'=2,'sub'=2] {'tile','view','sub'}, dimensions={1} | all-to-all | bytes 524288 | tf_op jit(solution)/shard_map/all_to_all | solution.py:535
  77.7 0.0 copy-start.5
  77.7 0.0 copy-start.7
  77.7 0.0 copy-done.1
  77.7 0.8 copy-done.5
  78.5 0.0 copy-done.7
  78.5 6.0 %owner_gradient.1 = (f32[58,4096]{1,0:T(8,128)}, f32[1,12]{1,0:T(1,128)}) custom-call(f32[3,4096]{1,0:T(4,128)S(1)} %copy-done.2, f32[3,4096]{1,0:T(4,128)S(1)} %copy-done.3, f32[3,4096]{1,0:T(4,128)S(1)} %copy-done.5, f32[1,4096]{1,0:T(1,128)S(1)} %bitcast.92, f32[48,4096]{1,0:T(8,128)S(1)} %copy-done.1, f32[2,8]{1,0:T(2,128)S(1)} %copy-done.8, ...), custom_call_target="tpu_custom_call" | custom-call | tf_op jit(solution)/shard_map/owner_gradient/pallas_call | solution.py:604
  (7 shorter events, 0.1 us)
Async XLA Ops:
  0.6 1.7 %copy-start.8 = (f32[2,8]{1,0:T(2,128)S(1)}, f32[2,8]{1,0:T(2,128)}, u32[]{:S(2)}) copy-start(f32[2,8]{1,0:T(2,128)} %cameras_ref.3) | copy-start | bytes 196
  1.5 1.3 %copy-start.2 = (f32[3,4096]{1,0:T(4,128)S(1)}, f32[3,4096]{1,0:T(4,128)}, u32[]{:S(2)}) copy-start(f32[3,4096]{1,0:T(4,128)} %centers_ref.3) | copy-start | bytes 147460
  1.6 1.3 %copy-start.3 = (f32[3,4096]{1,0:T(4,128)S(1)}, f32[3,4096]{1,0:T(4,128)}, u32[]{:S(2)}) copy-start(f32[3,4096]{1,0:T(4,128)} %scale_ref.3) | copy-start | bytes 147460
  2.9 0.7 copy-start.11
  3.5 1.1 %copy-start = (f32[48,4096]{1,0:T(8,128)S(1)}, f32[48,4096]{1,0:T(8,128)}, u32[]{:S(2)}) copy-start(f32[48,4096]{1,0:T(8,128)} %coeff_ref.3) | copy-start | bytes 2359300
  4.6 0.8 copy-start.4
  5.5 0.7 copy-start.6
  33.3 0.7 copy-start.9
  33.3 0.7 copy-start.10
  33.3 0.7 copy-start.12
  33.3 0.7 copy-start.13
  64.7 13.0 %copy-start.1 = (f32[48,4096]{1,0:T(8,128)S(1)}, f32[48,4096]{1,0:T(8,128)}, u32[]{:S(2)}) copy-start(f32[48,4096]{1,0:T(8,128)} %coeff_ref.3) | copy-start | bytes 2359300
  77.7 0.8 copy-start.5
  77.7 0.8 copy-start.7
where the time goes:
time: 85.1 us; the launch traced here: 84.5 us
  Pallas kernels  46.5 us (55%)
  blocking collectives  30.2 us (35%)
  local copies, waits for them, and re-layouts  5.74 us (7%)
  other arithmetic  1.35 us (2%)
    pallas_call x1, Pallas kernels, on_device(): pl.pallas_call(functools.partial(tile_kernel, slot_cap, peers, sub_count)...  30.7 us
    all_to_all x2, blocking collectives, exchange(): lax.all_to_all(rows, ROUTE_AXES, split_axis=1, concat_axis=1, tiled=True)  30.2 us
    pallas_call x1, Pallas kernels, on_device(): pl.pallas_call(functools.partial(owner_kernel, sub_count, view_count, slo...  9.85 us
    pallas_call x1, Pallas kernels, on_device(): pl.pallas_call(functools.partial(gradient_kernel, sub_count, view_count,...  6.01 us
    unnamed x28, local copies, waits for them, and re-layouts  4.85 us

commit v1 on v0

--- a/solution.py
+++ b/solution.py
@@ -97,44 +97,79 @@
     return lax.broadcasted_iota(I32, shape, dim)
 
 
-def onehot_scatter(total, high, low, first, second, live):
-    blocks = total.shape[0] // 2
-    hit = iota((blocks, LANES), 0) == high
-    if live is not None:
-        hit = jnp.logical_and(hit, live)
-    left = jnp.concatenate(
-        [jnp.where(hit, first, 0.0), jnp.where(hit, second, 0.0)], axis=0
-    ).astype(BF16)
-    right = (iota((LANES, LANES), 0) == low).astype(F32).astype(BF16)
-    return total + lax.dot_general(left, right, NT, preferred_element_type=F32)
-
-
-def gather_columns(out_ref, source_ref, high_ref, low_ref):
-    out_blocks = high_ref.shape[0]
-    blocks = source_ref.shape[1] // LANES
-
-    def one_block(place, carry):
-        high = spread(high_ref[pl.ds(place, 1), :], 8)
-        low = spread(low_ref[pl.ds(place, 1), :], 8)
-        found = jnp.zeros((8, LANES), F32)
-        for block in range(blocks):
-            cut = slice(block * LANES, (block + 1) * LANES)
-            found = jnp.where(high == block, lane_gather(source_ref[0:8, cut], low), found)
-        out_ref[0:8, pl.ds(pl.multiple_of(place * LANES, LANES), LANES)] = found
-        return carry
-
-    lax.fori_loop(0, out_blocks, one_block, 0)
-    for group in range(out_blocks // 8):
+def divide(values, number):
+    if number & (number - 1) == 0:
+        return values >> (number.bit_length() - 1)
+    return lax.div(values, jnp.full_like(values, number))
+
+
+def inverse_table(blocks, items):
+    total = jnp.zeros((2 * blocks, LANES), F32)
+    group = 8
+    for start in range(0, len(items), group):
+        lefts, rights = [], []
+        for high, low, first, second, live in items[start : start + group]:
+            hit = iota((blocks, LANES), 0) == high
+            if live is not None:
+                hit = jnp.logical_and(hit, live)
+            lefts.append(
+                jnp.concatenate([jnp.where(hit, first, 0.0), jnp.where(hit, second, 0.0)], axis=0)
+            )
+            rights.append((iota((LANES, LANES), 0) == low).astype(F32))
+        left = jnp.concatenate(lefts, axis=1).astype(BF16)
+        right = jnp.concatenate(rights, axis=1).astype(BF16)
+        total = total + lax.dot_general(left, right, NT, preferred_element_type=F32)
+    return total.astype(I32)
+
+
+def gather_columns(high_ref, low_ref, blocks, tile_of, ninth_of, finish, finish_ninth):
+    places = high_ref.shape[0]
+    together = 4
+    for group in range(places // 8):
         high = high_ref[group * 8 : group * 8 + 8, :]
         low = low_ref[group * 8 : group * 8 + 8, :]
         found = jnp.zeros((8, LANES), F32)
         for block in range(blocks):
-            cut = slice(block * LANES, (block + 1) * LANES)
-            row = spread(source_ref[8:9, cut], 8)
-            found = jnp.where(high == block, lane_gather(row, low), found)
+            found = jnp.where(high == block, lane_gather(spread(ninth_of(block), 8), low), found)
         for inner in range(8):
-            place = group * 8 + inner
-            out_ref[8:9, place * LANES : (place + 1) * LANES] = found[inner : inner + 1, :]
+            finish_ninth(group * 8 + inner, found[inner : inner + 1, :])
+
+    def some_blocks(number, carry):
+        first = number * together
+        high = [spread(high_ref[pl.ds(first + n, 1), :], 8) for n in range(together)]
+        low = [spread(low_ref[pl.ds(first + n, 1), :], 8) for n in range(together)]
+        found = [jnp.zeros((8, LANES), F32) for _ in range(together)]
+        for block in range(blocks):
+            values = tile_of(block)
+            for n in range(together):
+                found[n] = jnp.where(high[n] == block, lane_gather(values, low[n]), found[n])
+        for n in range(together):
+            finish(first + n, found[n], low[n])
+        return carry
+
+    lax.fori_loop(0, places // together, some_blocks, 0)
+
+
+class Packet:
+    def __init__(self, ref, slot_cap):
+        self.ref = ref
+        self.cap = slot_cap
+        self.deep = max(slot_cap // LANES, 1)
+
+    def tile(self, block):
+        start = (block % self.deep) * 8
+        if not isinstance(block, int):
+            start = pl.multiple_of(start, 8)
+        return (block // self.deep, pl.ds(start, 8), slice(None))
+
+    def row(self, block, number):
+        start = (block % self.deep) * 8 + number if number < 8 else self.deep * 8 + block % self.deep
+        return (block // self.deep, slice(start, start + 1), slice(None))
+
+    def extra(self, peer):
+        start = peer * self.cap
+        lanes = slice(start % LANES, start % LANES + min(self.cap, LANES))
+        return (start // LANES // self.deep, slice(9 * self.deep, 9 * self.deep + 1), lanes)
 
 
 def select_camera(cameras_ref, view):
@@ -177,34 +212,31 @@
     low_ref,
     projected_ref,
 ):
-    blocks = slots_ref.shape[0]
-    slots = slots_ref[...]
-    high_ref[...] = slots >> 7
-    low_ref[...] = slots & 127
+    blocks = high_ref.shape[0]
+    wide = slots_ref.shape[1] // LANES
     peers = count_ref.shape[1]
-
-    lane = iota((blocks, LANES), 1)
-
-    def one_block(place, total):
-        return onehot_scatter(
-            total,
-            high_ref[pl.ds(place, 1), :],
-            low_ref[pl.ds(place, 1), :],
-            place.astype(F32),
-            lane.astype(F32),
-            None,
-        )
-
-    table = lax.fori_loop(0, blocks, one_block, jnp.zeros((2 * blocks, LANES), F32)).astype(I32)
+    packet = Packet(out_ref, slot_cap)
+    lane = iota((1, LANES), 1).astype(F32)
+    items = []
+    for block in range(blocks):
+        cut = slice((block % wide) * LANES, (block % wide + 1) * LANES)
+        row = slots_ref[block // wide : block // wide + 1, cut]
+        high = row >> 7
+        low = row & 127
+        high_ref[block : block + 1, :] = high
+        low_ref[block : block + 1, :] = low
+        items.append((high, low, float(block), lane, None))
+    table = inverse_table(blocks, items)
     place_ref[...] = table
     position = table[0:blocks] * LANES + table[blocks:]
-    dest = position // slot_cap
-    view = (dest // sub_count) % view_count
+    dest = divide(position, slot_cap)
+    view = lax.rem(divide(dest, sub_count), jnp.full_like(dest, view_count))
     within = position - dest * slot_cap
     limit = jnp.zeros_like(dest)
     for peer in range(peers):
         limit = jnp.where(dest == peer, count_ref[0, peer], limit)
-    live = (within < limit).astype(I32)
+    live = (within < limit).astype(F32)
+    view = view.astype(F32)
     for block in range(blocks):
         cut = slice(block * LANES, (block + 1) * LANES)
         owner_ref[0:1, cut] = view[block : block + 1, :]
@@ -223,17 +255,34 @@
         basis = select_harmonics(harmonics_ref, view_row)
         for color in range(3):
             terms = coeff_ref[color * 16 : color * 16 + 16, cut] * basis
-            rows.append(jnp.maximum(jnp.sum(terms, axis=0, keepdims=True) + 0.5, 0.0))
+            value = jnp.sum(terms, axis=0, keepdims=True) + 0.5
+            slope = jnp.where(value > 0.0, 1.0, jnp.where(value == 0.0, 0.5, 0.0))
+            owner_ref[2 + color : 3 + color, cut] = slope
+            rows.append(jnp.maximum(value, 0.0))
         for row in range(9):
             projected_ref[row : row + 1, cut] = rows[row]
         return carry
 
     lax.fori_loop(0, coeff_ref.shape[1] // step, one_chunk, 0)
-    out_ref[8:16, :] = jnp.zeros((8, out_ref.shape[1]), F32)
-    gather_columns(out_ref, projected_ref, high_ref, low_ref)
+
+    def tile_of(block):
+        return projected_ref[0:8, block * LANES : (block + 1) * LANES]
+
+    def ninth_of(block):
+        return projected_ref[8:9, block * LANES : (block + 1) * LANES]
+
+    def finish(place, found, low):
+        out_ref[packet.tile(place)] = found
+
+    def finish_ninth(place, found):
+        out_ref[packet.row(place, 8)] = found
+
+    gather_columns(
+        high_ref, low_ref, projected_ref.shape[1] // LANES, tile_of, ninth_of, finish, finish_ninth
+    )
     for peer in range(peers):
-        out_ref[9:10, peer * slot_cap : (peer + 1) * slot_cap] = jnp.full(
-            (1, slot_cap), count_ref[0, peer].astype(F32)
+        out_ref[packet.extra(peer)] = jnp.full(
+            (1, min(slot_cap, LANES)), count_ref[0, peer].astype(F32)
         )
 
 
@@ -252,13 +301,14 @@
     alpha_ref,
     weight_ref,
     moment_ref,
-    gathered_ref,
     high_ref,
     low_ref,
 ):
     tiles, list_len = list_ref.shape
     tile_pix = target_ref.shape[2]
-    blocks = pool_ref.shape[1] // LANES
+    blocks = high_ref.shape[0]
+    pool = Packet(pool_ref, slot_cap)
+    packet = Packet(out_ref, slot_cap)
     cols = list_len // LANES
     halves = tile_pix // LANES
     tile_row = lax.axis_index("tile") * sub_count + lax.axis_index("sub")
@@ -268,13 +318,15 @@
     column = entries
     inclusive = jnp.zeros((1, LANES), I32)
     for peer in range(peers):
-        start = peer * slot_cap
-        received = jnp.broadcast_to(pool_ref[9:10, start : start + 1], (1, LANES)).astype(I32)
+        received = pool_ref[pool.extra(peer)]
+        if slot_cap < LANES:
+            received = jnp.broadcast_to(received[:, 0:1], (1, LANES))
+        received = received.astype(I32)
         inclusive = inclusive + received
         bound = jnp.concatenate([spread(inclusive, tiles)] * cols, axis=1)
         gap = jnp.concatenate([spread(slot_cap - received, tiles)] * cols, axis=1)
         column = column + jnp.where(bound <= entries, gap, 0)
-    column = jnp.clip(column, 0, pool_ref.shape[1] - 1)
+    column = jnp.clip(column, 0, blocks * LANES - 1)
     lane = iota((tiles, list_len), 1)
     tile = iota((tiles, list_len), 0)
     live_limit = jnp.zeros((tiles, list_len), I32)
@@ -293,7 +345,7 @@
         for block in range(blocks):
             hit = high == block
             for row in range(9):
-                source = spread(pool_ref[row : row + 1, block * LANES : (block + 1) * LANES], tiles)
+                source = spread(pool_ref[pool.row(block, row)], tiles)
                 found[row] = jnp.where(hit, lane_gather(source, low), found[row])
         found[0] = found[0] - tile_x
         found[1] = found[1] - center_y
@@ -357,8 +409,8 @@
         for d in range(3)
     ]
     sums = [residue[c] * blended[d] for c in range(3) for d in range(3)] + residue
-    term_lane = iota((1, slot_cap), 1)
-    term_row = jnp.zeros((1, slot_cap), F32)
+    term_lane = iota((1, min(slot_cap, LANES)), 1)
+    term_row = jnp.zeros((1, min(slot_cap, LANES)), F32)
     for number, values in enumerate(sums):
         total = jnp.sum(jnp.sum(values, axis=0, keepdims=True), axis=1, keepdims=True)
         term_row = jnp.where(term_lane == number, total, term_row)
@@ -428,51 +480,66 @@
 
     lax.fori_loop(0, list_len // steps, reduce_pixels, 0)
 
-    table = jnp.zeros((2 * blocks, LANES), F32)
+    items = []
     place_lane = iota((1, LANES), 1)
     for number in range(tiles):
         for col in range(cols):
             cut = slice(col * LANES, (col + 1) * LANES)
             k = place_lane + col * LANES
             flat = k * tiles + number
-            table = onehot_scatter(
-                table,
-                high_all[number : number + 1, cut],
-                low_all[number : number + 1, cut],
-                (flat >> 7).astype(F32),
-                (flat & 127).astype(F32),
-                k < count_ref[0, number],
+            items.append(
+                (
+                    high_all[number : number + 1, cut],
+                    low_all[number : number + 1, cut],
+                    (flat >> 7).astype(F32),
+                    (flat & 127).astype(F32),
+                    k < count_ref[0, number],
+                )
             )
-    table = table.astype(I32)
+    table = inverse_table(blocks, items)
     high_ref[...] = table[0:blocks]
     low_ref[...] = table[blocks:]
-    gather_columns(gathered_ref, moment_ref, high_ref, low_ref)
-
-    for block in range(blocks):
-        cut = slice(block * LANES, (block + 1) * LANES)
-        own = (table[blocks + block : blocks + block + 1, :] & (tiles - 1)).astype(F32)
-        local_x = pool_ref[0:1, cut] - (16.0 * own + 7.5)
-        local_y = pool_ref[1:2, cut] - center_y
-        conic_a = pool_ref[2:3, cut]
-        conic_b = pool_ref[3:4, cut]
-        conic_c = pool_ref[4:5, cut]
-        one, m_x, m_y, m_xx, m_xy, m_yy = [gathered_ref[r : r + 1, cut] for r in range(6)]
+
+    def tile_of(block):
+        return moment_ref[0:8, block * LANES : (block + 1) * LANES]
+
+    def ninth_of(block):
+        return moment_ref[8:9, block * LANES : (block + 1) * LANES]
+
+    def finish(place, found, low):
+        at = packet.tile(place)
+        own = (low[0:1] & (tiles - 1)).astype(F32)
+        shape = pool_ref[at]
+        local_x = shape[0:1] - (16.0 * own + 7.5)
+        local_y = shape[1:2] - center_y
+        conic_a, conic_b, conic_c = shape[2:3], shape[3:4], shape[4:5]
+        one, m_x, m_y, m_xx, m_xy, m_yy = [found[r : r + 1] for r in range(6)]
         d_x = local_x * one - m_x
         d_y = local_y * one - m_y
         d_xx = local_x * d_x - (local_x * m_x - m_xx)
         d_xy = local_y * d_x - (local_x * m_y - m_xy)
         d_yy = local_y * d_y - (local_y * m_y - m_yy)
-        out_ref[0:1, cut] = -(conic_a * d_x + conic_b * d_y)
-        out_ref[1:2, cut] = -(conic_c * d_y + conic_b * d_x)
-        out_ref[2:3, cut] = -0.5 * d_xx
-        out_ref[3:4, cut] = -d_xy
-        out_ref[4:5, cut] = -0.5 * d_yy
-        out_ref[5:6, cut] = one
-    out_ref[6:8, :] = gathered_ref[6:8, :]
-    out_ref[8:16, :] = jnp.zeros((8, out_ref.shape[1]), F32)
-    out_ref[8:9, :] = gathered_ref[8:9, :]
+        out_ref[at] = jnp.concatenate(
+            [
+                -(conic_a * d_x + conic_b * d_y),
+                -(conic_c * d_y + conic_b * d_x),
+                -0.5 * d_xx,
+                -d_xy,
+                -0.5 * d_yy,
+                one,
+                found[6:8],
+            ],
+            axis=0,
+        )
+
+    def finish_ninth(place, found):
+        out_ref[packet.row(place, 8)] = found
+
+    gather_columns(
+        high_ref, low_ref, moment_ref.shape[1] // LANES, tile_of, ninth_of, finish, finish_ninth
+    )
     for peer in range(peers):
-        out_ref[9:10, peer * slot_cap : (peer + 1) * slot_cap] = term_row
+        out_ref[packet.extra(peer)] = term_row
 
 
 def gradient_kernel(
@@ -485,7 +552,6 @@
     scale_ref,
     shear_ref,
     opacity_ref,
-    coeff_ref,
     cameras_ref,
     harmonics_ref,
     place_ref,
@@ -498,15 +564,29 @@
     low_ref,
 ):
     blocks = high_ref.shape[0]
+    packet = Packet(back_ref, slot_cap)
     high_ref[...] = place_ref[0:blocks, :]
     low_ref[...] = place_ref[blocks:, :]
-    gather_columns(gathered_ref, back_ref, high_ref, low_ref)
+
+    def tile_of(block):
+        return back_ref[packet.tile(block)]
+
+    def ninth_of(block):
+        return back_ref[packet.row(block, 8)]
+
+    def finish(place, found, low):
+        gathered_ref[0:8, pl.ds(pl.multiple_of(place * LANES, LANES), LANES)] = found
+
+    def finish_ninth(place, found):
+        gathered_ref[8:9, place * LANES : (place + 1) * LANES] = found
+
+    gather_columns(high_ref, low_ref, blocks, tile_of, ninth_of, finish, finish_ninth)
     step = 512
 
     def one_chunk(number, carry):
         cut = pl.ds(pl.multiple_of(number * step, step), step)
         view_row = owner_ref[0:1, cut]
-        live = owner_ref[1:2, cut] > 0
+        live = owner_ref[1:2, cut] > 0.0
         grads = [jnp.where(live, gathered_ref[r : r + 1, cut], 0.0) for r in range(9)]
         camera = select_camera(cameras_ref, view_row)
         params = [ref[r : r + 1, cut] for ref in (centers_ref, scale_ref, shear_ref) for r in range(3)]
@@ -516,23 +596,82 @@
         out_ref[9:10, cut] = grads[5] / (1.0 + jnp.exp(opacity_ref[0:1, cut]))
         basis = select_harmonics(harmonics_ref, view_row)
         for color in range(3):
-            terms = coeff_ref[color * 16 : color * 16 + 16, cut] * basis
-            value = jnp.sum(terms, axis=0, keepdims=True) + 0.5
-            slope = jnp.where(value > 0.0, 1.0, jnp.where(value == 0.0, 0.5, 0.0))
+            slope = owner_ref[2 + color : 3 + color, cut]
             out_ref[10 + 16 * color : 26 + 16 * color, cut] = basis * (slope * grads[6 + color])
         return carry
 
-    lax.fori_loop(0, coeff_ref.shape[1] // step, one_chunk, 0)
+    lax.fori_loop(0, out_ref.shape[1] // step, one_chunk, 0)
     mine = lax.axis_index("view")
-    total = jnp.zeros((1, slot_cap), F32)
+    total = jnp.zeros((1, min(slot_cap, LANES)), F32)
     for peer in range(peers):
         same = ((peer // sub_count) % view_count == mine).astype(F32)
-        total = total + same * back_ref[9:10, peer * slot_cap : (peer + 1) * slot_cap]
+        total = total + same * back_ref[packet.extra(peer)]
     appear_ref[...] = (total * (1.0 / pixels))[:, :12]
 
 
-def exchange(rows):
-    return lax.all_to_all(rows, ROUTE_AXES, split_axis=1, concat_axis=1, tiled=True)
+def exchange_kernel(view_count, sub_count, in_ref, out_ref, send_sem, recv_sem, own_sem):
+    peers = in_ref.shape[0]
+    me = (lax.axis_index("tile") * view_count + lax.axis_index("view")) * sub_count
+    me = me + lax.axis_index("sub")
+
+    def device(number):
+        return {
+            "tile": number // (view_count * sub_count),
+            "view": (number // sub_count) % view_count,
+            "sub": number % sub_count,
+        }
+
+    barrier = pltpu.get_barrier_semaphore()
+    for offset in range(1, peers):
+        pl.semaphore_signal(
+            barrier,
+            inc=1,
+            device_id=device((me + offset) % peers),
+            device_id_type=pl.DeviceIdType.MESH,
+        )
+    own = pltpu.make_async_copy(in_ref.at[me], out_ref.at[me], own_sem)
+    own.start()
+    pl.semaphore_wait(barrier, peers - 1)
+    copies = []
+    for offset in sorted(range(1, peers), key=lambda n: abs(2 * n - peers)):
+        dest = (me + offset) % peers
+        copy = pltpu.make_async_remote_copy(
+            src_ref=in_ref.at[dest],
+            dst_ref=out_ref.at[me],
+            send_sem=send_sem.at[offset],
+            recv_sem=recv_sem.at[offset],
+            device_id=device(dest),
+            device_id_type=pl.DeviceIdType.MESH,
+        )
+        copy.start()
+        copies.append(copy)
+    own.wait()
+    for copy in copies:
+        copy.wait()
+
+
+def exchange(packets, number, peers, slot_cap):
+    view_count = lax.axis_size("view")
+    sub_count = lax.axis_size("sub")
+    if slot_cap % LANES:
+        blocks = packets.shape[0]
+        rows = packets[:, :10].transpose(1, 0, 2).reshape(10, blocks * LANES)
+        rows = lax.all_to_all(rows, ROUTE_AXES, split_axis=1, concat_axis=1, tiled=True)
+        rows = rows.reshape(10, blocks, LANES).transpose(1, 0, 2)
+        return jnp.pad(rows, ((0, 0), (0, 6), (0, 0)))
+    return pl.pallas_call(
+        functools.partial(exchange_kernel, view_count, sub_count),
+        out_shape=jax.ShapeDtypeStruct(packets.shape, F32),
+        in_specs=[IN_VMEM],
+        out_specs=IN_VMEM,
+        scratch_shapes=[
+            pltpu.SemaphoreType.DMA((peers,)),
+            pltpu.SemaphoreType.DMA((peers,)),
+            pltpu.SemaphoreType.DMA,
+        ],
+        compiler_params=pltpu.CompilerParams(collective_id=number, has_side_effects=True),
+        name="exchange",
+    )(packets)
 
 
 def on_device(
@@ -560,16 +699,21 @@
     tile_devs = lax.axis_size("tile")
     harmonics = harmonic_table(cameras)
     opacity_row = opacity_logit[None, :]
-    source = (centers, scale_log, shear_terms, opacity_row, sh_coeffs, cameras, harmonics)
-    source_specs = [IN_VMEM] * 5 + [IN_SMEM, IN_VMEM]
+    source = (centers, scale_log, shear_terms, opacity_row)
+    deep = max(slot_cap // LANES, 1)
+    packet_shape = jax.ShapeDtypeStruct((blocks // deep, 8 * deep + 8, LANES), F32)
+    if slot_cap % LANES:
+        slot_rows = send_index.reshape(blocks, LANES)
+    else:
+        slot_rows = send_index[0]
     outgoing, place, owner = pl.pallas_call(
         functools.partial(owner_kernel, sub_count, view_count, slot_cap),
         out_shape=(
-            jax.ShapeDtypeStruct((16, slots), F32),
+            packet_shape,
             jax.ShapeDtypeStruct((2 * blocks, LANES), I32),
-            jax.ShapeDtypeStruct((8, gauss_count), I32),
+            jax.ShapeDtypeStruct((8, gauss_count), F32),
         ),
-        in_specs=source_specs + [IN_VMEM, IN_SMEM],
+        in_specs=[IN_VMEM] * 5 + [IN_SMEM, IN_VMEM, IN_VMEM, IN_SMEM],
         out_specs=(IN_VMEM,) * 3,
         scratch_shapes=[
             pltpu.VMEM((blocks, LANES), I32),
@@ -578,12 +722,12 @@
         ],
         compiler_params=PARAMS,
         name="owner_rows",
-    )(*source, send_index.reshape(blocks, LANES), send_count)
-    arrived = exchange(outgoing)
+    )(*source, sh_coeffs, cameras, harmonics, slot_rows, send_count)
+    arrived = exchange(outgoing, 0, peers, slot_cap)
     returning, rendered = pl.pallas_call(
         functools.partial(tile_kernel, slot_cap, peers, sub_count),
         out_shape=(
-            jax.ShapeDtypeStruct((16, slots), F32),
+            packet_shape,
             jax.ShapeDtypeStruct((3, tiles, tile_pix), F32),
         ),
         in_specs=[IN_VMEM, IN_VMEM, IN_SMEM, IN_SMEM, IN_VMEM],
@@ -593,14 +737,13 @@
             pltpu.VMEM((list_len, tiles, tile_pix), F32),
             pltpu.VMEM((list_len, tiles, tile_pix), F32),
             pltpu.VMEM((16, tiles * list_len), F32),
-            pltpu.VMEM((16, slots), F32),
             pltpu.VMEM((blocks, LANES), I32),
             pltpu.VMEM((blocks, LANES), I32),
         ],
         compiler_params=PARAMS,
         name="tile_blend",
     )(arrived, tile_list[0], tile_count, appearance, target[:, 0, 0])
-    returned = exchange(returning)
+    returned = exchange(returning, 1, peers, slot_cap)
     param_grad, appearance_grad = pl.pallas_call(
         functools.partial(
             gradient_kernel,
@@ -614,7 +757,7 @@
             jax.ShapeDtypeStruct((10 + sh_coeffs.shape[0], gauss_count), F32),
             jax.ShapeDtypeStruct((1, 12), F32),
         ),
-        in_specs=source_specs + [IN_VMEM] * 3,
+        in_specs=[IN_VMEM] * 4 + [IN_SMEM] + [IN_VMEM] * 4,
         out_specs=(IN_VMEM,) * 2,
         scratch_shapes=[
             pltpu.VMEM((16, gauss_count), F32),
@@ -623,7 +766,7 @@
         ],
         compiler_params=PARAMS,
         name="owner_gradient",
-    )(*source, place, owner, returned)
+    )(*source, cameras, harmonics, place, owner, returned)
     return (rendered[:, None, None], param_grad, appearance_grad)
 
 

time: 85.1 us -> 75.7 us (0.89)
  blocking collectives: 30.2 us -> 0 us
  Pallas kernels: 46.5 us -> 65.6 us
  local copies, waits for them, and re-layouts: 5.74 us -> 6.73 us
    all_to_all x2 -> x0, blocking collectives: 30.2 us -> none  [exchange(): lax.all_to_all(rows, ROUTE_AXES, split_axis=1, concat_axis=1, tiled=True)]
    pallas_call x0 -> x2, Pallas kernels: none -> 23.8 us  [exchange(): pl.pallas_call(functools.partial(exchange_kernel, view_count, sub_count),...]
    pallas_call x1, Pallas kernels: 9.85 us -> 5.46 us  [on_device(): pl.pallas_call(functools.partial(owner_kernel, sub_count, view_count, slo...]
    unnamed x28 -> x36, local copies, waits for them, and re-layouts: 4.85 us -> 6.67 us
where the time goes in v1:
time: 75.7 us; the launch traced here: 75.3 us
  Pallas kernels  65.6 us (87%)
  local copies, waits for them, and re-layouts  6.73 us (9%)
  other arithmetic  2.09 us (3%)
  between operations  0.81 us (1%)
    pallas_call x1, Pallas kernels, on_device(): pl.pallas_call(functools.partial(tile_kernel, slot_cap, peers, sub_count)...  30.6 us
    pallas_call x2, Pallas kernels, exchange(): pl.pallas_call(functools.partial(exchange_kernel, view_count, sub_count),...  23.8 us
    unnamed x36, local copies, waits for them, and re-layouts  6.67 us
    pallas_call x1, Pallas kernels, on_device(): pl.pallas_call(functools.partial(gradient_kernel, sub_count, view_count,...  5.73 us
    pallas_call x1, Pallas kernels, on_device(): pl.pallas_call(functools.partial(owner_kernel, sub_count, view_count, slo...  5.46 us

profile of v1, /device:TPU:0, one launch (start us, length us, event | category | flops | bytes accessed | tf_op | source)
XLA Modules:
  0.0 75.3 jit_solution(1694238137700825063)
XLA Ops:
  0.6 0.0 copy-start.3
  0.6 0.9 %sine_multiply_fusion = (f32[2,1]{1,0:T(2,128)S(1)}, f32[2,1]{1,0:T(2,128)S(1)}) fusion(f32[2,8]{1,0:T(2,128)} %cameras_ref.3), kind=kLoop, calls=%fused_computation.18 | loop fusion | flops 4 | bytes 32 | tf_op jit(solution)/shard_map/mul | solution.py:26
  1.5 1.2 %multiply_reduce_fusion.8 = (f32[2]{0:T(128)S(1)}, f32[2]{0:T(128)S(1)}, f32[2]{0:T(128)S(1)}, f32[2]{0:T(128)S(1)}, f32[2]{0:T(128)S(1)}, /*index=5*/f32[2]{0:T...) fusion(f32[2,1]{1,0:T(2,128)S(1)} %get-tuple-element.60, ...), kind=kLoop, calls=%fused_computation.8 | loop fusion | flops 46 | bytes 160 | tf_op jit(solution)/shard_map/mul | solution.py:47
  2.7 0.0 copy-start.15
  2.7 0.0 copy-start.13
  2.8 0.0 copy-start.10
  2.8 0.0 copy-start.11
  2.8 0.1 stack.2.harmonics_ref
  2.9 0.0 copy-done.3
  2.9 0.5 copy-done.15
  3.4 0.1 copy-done.13
  3.5 0.0 copy-done.10
  3.5 0.0 copy-done.11
  3.5 0.0 copy-start
  3.5 1.1 %copy-done = f32[48,4096]{1,0:T(8,128)S(1)} copy-done((f32[48,4096]{1,0:T(8,128)S(1)}, f32[48,4096]{1,0:T(8,128)}, u32[]{:S(2)}) %copy-start) | copy-done | bytes 786456
  4.6 0.0 copy-start.4
  4.6 0.8 %copy-done.4 = f32[3,4096]{1,0:T(4,128)S(1)} copy-done((f32[3,4096]{1,0:T(4,128)S(1)}, f32[3,4096]{1,0:T(4,128)}, u32[]{:S(2)}) %copy-start.4) | copy-done | bytes 49176
  5.5 0.0 copy-start.6
  5.5 0.8 %copy-done.6 = f32[3,4096]{1,0:T(4,128)S(1)} copy-done((f32[3,4096]{1,0:T(4,128)S(1)}, f32[3,4096]{1,0:T(4,128)}, u32[]{:S(2)}) %copy-start.6) | copy-done | bytes 49176
  6.3 5.5 %owner_rows.1 = (f32[16,24,128]{2,1,0:T(8,128)S(1)}, s32[64,128]{1,0:T(8,128)S(1)}, f32[8,4096]{1,0:T(8,128)S(1)}) custom-call(f32[3,4096]{1,0:T(4,128)S(1)} %copy-done.3, f32[3,4096]{1,0:T(4,128)S(1)} %copy-done.4, f32[3,4096]{1,0:T(4,128)S(1)} %copy-done.6, f32[1,4096]{1,0:T(1,128)S(1)} %bitcast.76, f32[48,4096]{1,0:T(8,128)S(1)} %copy-done, ...), custom_call_target="tpu_custom_call" | custom-call | tf_op jit(solution)/shard_map/owner_rows/pallas_call | solution.py:709
  11.8 0.0 copy-start.8
  11.8 0.7 copy-done.8
  12.5 0.0 copy-start.12
  12.5 0.0 copy-start.14
  12.5 0.0 copy-start.16
  12.5 0.0 copy-start.17
  12.5 13.0 %exchange.2.pool_ref = f32[16,24,128]{2,1,0:T(8,128)} custom-call(f32[16,24,128]{2,1,0:T(8,128)} %copy-done.8), custom_call_target="tpu_custom_call" | custom-call | tf_op jit(solution)/shard_map/exchange/pallas_call | solution.py:662
  25.5 0.0 copy-done.12
  25.5 0.0 copy-done.14
  25.5 0.0 copy-done.16
  25.5 0.0 copy-done.17
  25.5 0.0 copy-start.2
  25.5 0.9 %copy-done.2 = f32[16,24,128]{2,1,0:T(8,128)S(1)} copy-done((f32[16,24,128]{2,1,0:T(8,128)S(1)}, f32[16,24,128]{2,1,0:T(8,128)}, u32[]{:S(2)}) %copy-start.2) | copy-done | bytes 196632
  26.5 30.6 %tile_blend.1 = (f32[16,24,128]{2,1,0:T(8,128)S(1)}, f32[3,8,256]{2,1,0:T(8,128)}) custom-call(f32[16,24,128]{2,1,0:T(8,128)S(1)} %copy-done.2, s32[8,512]{1,0:T(8,128)S(1)} %bitcast.80, s32[1,8]{1,0:T(1,128)S(1)} %copy-done.16, f32[1,12]{1,0:T(1,128)S(1)} %copy-done.17, f32[3,8,256]{2,1,0:T(8,128)S(1)} %bitcast.78), custom_call_target="tpu_custom_call" | custom-call | tf_op jit(solution)/shard_map/tile_blend/pallas_call | solution.py:727
  57.1 0.0 copy-start.9
  57.1 0.7 copy-done.9
  57.7 0.0 copy-start.5
  57.7 0.0 copy-start.7
  57.7 10.8 %exchange.3.back_ref = f32[16,24,128]{2,1,0:T(8,128)} custom-call(f32[16,24,128]{2,1,0:T(8,128)} %copy-done.9), custom_call_target="tpu_custom_call" | custom-call | tf_op jit(solution)/shard_map/exchange/pallas_call | solution.py:662
  68.6 0.0 copy-done.5
  68.6 0.0 copy-done.7
  68.6 0.0 copy-start.1
  68.6 0.9 %copy-done.1 = f32[16,24,128]{2,1,0:T(8,128)S(1)} copy-done((f32[16,24,128]{2,1,0:T(8,128)S(1)}, f32[16,24,128]{2,1,0:T(8,128)}, u32[]{:S(2)}) %copy-start.1) | copy-done | bytes 196632
  69.5 5.7 %owner_gradient.1 = (f32[58,4096]{1,0:T(8,128)}, f32[1,12]{1,0:T(1,128)}) custom-call(f32[3,4096]{1,0:T(4,128)S(1)} %copy-done.3, f32[3,4096]{1,0:T(4,128)S(1)} %copy-done.5, f32[3,4096]{1,0:T(4,128)S(1)} %copy-done.7, f32[1,4096]{1,0:T(1,128)S(1)} %bitcast.77, f32[2,8]{1,0:T(2,128)S(1)} %copy-done.11, f32[16,2]{1,0:T(8,128)S(1)} %stack.2.harmonics_ref, ...), custom_call_target="tpu_custom_call" | custom-call | tf_op jit(solution)/shard_map/owner_gradient/pallas_call | solution.py:747
  (3 shorter events, 0.0 us)
Async XLA Ops:
  0.6 2.2 %copy-start.3 = (f32[3,4096]{1,0:T(4,128)S(1)}, f32[3,4096]{1,0:T(4,128)}, u32[]{:S(2)}) copy-start(f32[3,4096]{1,0:T(4,128)} %centers_ref.3) | copy-start | bytes 147460
  2.7 0.7 copy-start.15
  2.7 0.7 copy-start.13
  2.8 0.7 copy-start.10
  2.8 0.7 copy-start.11
  3.5 1.1 %copy-start = (f32[48,4096]{1,0:T(8,128)S(1)}, f32[48,4096]{1,0:T(8,128)}, u32[]{:S(2)}) copy-start(f32[48,4096]{1,0:T(8,128)} %coeff_ref.1) | copy-start | bytes 2359300
  4.6 0.8 %copy-start.4 = (f32[3,4096]{1,0:T(4,128)S(1)}, f32[3,4096]{1,0:T(4,128)}, u32[]{:S(2)}) copy-start(f32[3,4096]{1,0:T(4,128)} %scale_ref.3) | copy-start | bytes 147460
  5.5 0.8 %copy-start.6 = (f32[3,4096]{1,0:T(4,128)S(1)}, f32[3,4096]{1,0:T(4,128)}, u32[]{:S(2)}) copy-start(f32[3,4096]{1,0:T(4,128)} %shear_ref.3) | copy-start | bytes 147460
  11.8 0.7 copy-start.8
  12.5 13.0 %copy-start.12 = (f32[3,1,1,8,256]{4,3,2,1,0:T(8,128)S(1)}, f32[3,1,1,8,256]{4,3,2,1,0:T(8,128)}, u32[]{:S(2)}) copy-start(f32[3,1,1,8,256]{4,3,2,1,0:T(8,128)} %param.19) | copy-start | bytes 73732
  12.5 13.0 %copy-start.14 = (s32[1,8,512]{2,1,0:T(8,128)S(1)}, s32[1,8,512]{2,1,0:T(8,128)}, u32[]{:S(2)}) copy-start(s32[1,8,512]{2,1,0:T(8,128)} %param.22) | copy-start | bytes 49156
  12.5 13.1 %copy-start.16 = (s32[1,8]{1,0:T(1,128)S(1)}, s32[1,8]{1,0:T(1,128)}, u32[]{:S(2)}) copy-start(s32[1,8]{1,0:T(1,128)} %count_ref.3) | copy-start | bytes 100
  12.5 13.1 %copy-start.17 = (f32[1,12]{1,0:T(1,128)S(1)}, f32[1,12]{1,0:T(1,128)}, u32[]{:S(2)}) copy-start(f32[1,12]{1,0:T(1,128)} %appear_ref.1) | copy-start | bytes 148
  25.5 0.9 %copy-start.2 = (f32[16,24,128]{2,1,0:T(8,128)S(1)}, f32[16,24,128]{2,1,0:T(8,128)}, u32[]{:S(2)}) copy-start(f32[16,24,128]{2,1,0:T(8,128)} %exchange.2.pool_ref) | copy-start | bytes 589828
  57.1 0.7 copy-start.9
  57.7 10.8 %copy-start.5 = (f32[3,4096]{1,0:T(4,128)S(1)}, f32[3,4096]{1,0:T(4,128)}, u32[]{:S(2)}) copy-start(f32[3,4096]{1,0:T(4,128)} %scale_ref.3) | copy-start | bytes 147460
  57.7 10.8 %copy-start.7 = (f32[3,4096]{1,0:T(4,128)S(1)}, f32[3,4096]{1,0:T(4,128)}, u32[]{:S(2)}) copy-start(f32[3,4096]{1,0:T(4,128)} %shear_ref.3) | copy-start | bytes 147460
  68.6 0.9 %copy-start.1 = (f32[16,24,128]{2,1,0:T(8,128)S(1)}, f32[16,24,128]{2,1,0:T(8,128)}, u32[]{:S(2)}) copy-start(f32[16,24,128]{2,1,0:T(8,128)} %exchange.3.back_ref) | copy-start | bytes 589828

commit v2 on v1

--- a/solution.py
+++ b/solution.py
@@ -16,6 +16,7 @@
 NT = (((1,), (1,)), ((), ()))
 PARAMS = pltpu.CompilerParams(vmem_limit_bytes=48 * 1024 * 1024)
 IN_VMEM = pl.BlockSpec(memory_space=pltpu.VMEM)
+IN_PLACE = pl.BlockSpec(memory_space=pl.ANY)
 IN_SMEM = pl.BlockSpec(memory_space=pltpu.SMEM)
 
 
@@ -196,11 +197,11 @@
     sub_count,
     view_count,
     slot_cap,
-    centers_ref,
-    scale_ref,
-    shear_ref,
-    opacity_ref,
-    coeff_ref,
+    centers_in,
+    scale_in,
+    shear_in,
+    opacity_in,
+    coeff_in,
     cameras_ref,
     harmonics_ref,
     slots_ref,
@@ -211,7 +212,27 @@
     high_ref,
     low_ref,
     projected_ref,
+    centers_ref,
+    scale_ref,
+    shear_ref,
+    opacity_ref,
+    coeff_ref,
+    load_sem,
 ):
+    loads = [
+        pltpu.make_async_copy(source, target, load_sem.at[number])
+        for number, (source, target) in enumerate(
+            (
+                (coeff_in, coeff_ref),
+                (centers_in, centers_ref),
+                (scale_in, scale_ref),
+                (shear_in, shear_ref),
+                (opacity_in, opacity_ref),
+            )
+        )
+    ]
+    for load in loads:
+        load.start()
     blocks = high_ref.shape[0]
     wide = slots_ref.shape[1] // LANES
     peers = count_ref.shape[1]
@@ -242,6 +263,8 @@
         owner_ref[0:1, cut] = view[block : block + 1, :]
         owner_ref[1:2, cut] = live[block : block + 1, :]
 
+    for load in loads:
+        load.wait()
     step = 512
 
     def one_chunk(number, carry):
@@ -387,7 +410,7 @@
                     new_colors.append(colors[half * 3 + color] + weight * row[6 + color])
             return (tuple(new_transmit), tuple(new_colors))
 
-        state = lax.fori_loop(0, LANES, forward, state, unroll=8)
+        state = lax.fori_loop(0, LANES, forward, state, unroll=32)
     blended = [
         jnp.concatenate([state[1][half * 3 + color] for half in range(halves)], axis=1)
         for color in range(3)
@@ -439,7 +462,7 @@
                 alpha_ref[col * LANES + k, :, cut] = ahead * weight_ref[col * LANES + k, :, cut]
             return tuple(new_behind)
 
-        behind = lax.fori_loop(0, LANES, backward, behind, unroll=8)
+        behind = lax.fori_loop(0, LANES, backward, behind, unroll=32)
 
     pix = iota((16, tile_pix), 1)
     mono_x = (pix & 15).astype(F32) - 7.5
@@ -662,8 +685,8 @@
     return pl.pallas_call(
         functools.partial(exchange_kernel, view_count, sub_count),
         out_shape=jax.ShapeDtypeStruct(packets.shape, F32),
-        in_specs=[IN_VMEM],
-        out_specs=IN_VMEM,
+        in_specs=[IN_PLACE],
+        out_specs=IN_PLACE,
         scratch_shapes=[
             pltpu.SemaphoreType.DMA((peers,)),
             pltpu.SemaphoreType.DMA((peers,)),
@@ -713,12 +736,18 @@
             jax.ShapeDtypeStruct((2 * blocks, LANES), I32),
             jax.ShapeDtypeStruct((8, gauss_count), F32),
         ),
-        in_specs=[IN_VMEM] * 5 + [IN_SMEM, IN_VMEM, IN_VMEM, IN_SMEM],
+        in_specs=[IN_PLACE] * 5 + [IN_SMEM, IN_VMEM, IN_VMEM, IN_SMEM],
         out_specs=(IN_VMEM,) * 3,
         scratch_shapes=[
             pltpu.VMEM((blocks, LANES), I32),
             pltpu.VMEM((blocks, LANES), I32),
             pltpu.VMEM((16, gauss_count), F32),
+            pltpu.VMEM(centers.shape, F32),
+            pltpu.VMEM(scale_log.shape, F32),
+            pltpu.VMEM(shear_terms.shape, F32),
+            pltpu.VMEM(opacity_row.shape, F32),
+            pltpu.VMEM(sh_coeffs.shape, F32),
+            pltpu.SemaphoreType.DMA((5,)),
         ],
         compiler_params=PARAMS,
         name="owner_rows",

time: 75.7 us -> 66.3 us (0.88)
  Pallas kernels: 65.6 us -> 56.2 us
    pallas_call x1, Pallas kernels: 30.6 us -> 23.3 us  [on_device(): pl.pallas_call(functools.partial(tile_kernel, slot_cap, peers, sub_count)...]
    pallas_call x2, Pallas kernels: 23.8 us -> 21.4 us  [exchange(): pl.pallas_call(functools.partial(exchange_kernel, view_count, sub_count),...]
where the time goes in v2:
time: 66.3 us; the launch traced here: 65.9 us
  Pallas kernels  56.2 us (85%)
  local copies, waits for them, and re-layouts  6.73 us (10%)
  other arithmetic  2.09 us (3%)
  between operations  0.81 us (1%)
    pallas_call x1, Pallas kernels, on_device(): pl.pallas_call(functools.partial(tile_kernel, slot_cap, peers, sub_count)...  23.3 us
    pallas_call x2, Pallas kernels, exchange(): pl.pallas_call(functools.partial(exchange_kernel, view_count, sub_count),...  21.4 us
    unnamed x36, local copies, waits for them, and re-layouts  6.67 us
    pallas_call x1, Pallas kernels, on_device(): pl.pallas_call(functools.partial(owner_kernel, sub_count, view_count, slo...  5.85 us
    pallas_call x1, Pallas kernels, on_device(): pl.pallas_call(functools.partial(gradient_kernel, sub_count, view_count,...  5.73 us

profile of v2, /device:TPU:0, one launch (start us, length us, event | category | flops | bytes accessed | tf_op | source)
XLA Modules:
  0.0 65.9 jit_solution(7016955753793643766)
XLA Ops:
  0.6 0.0 copy-start.3
  0.6 0.9 %sine_multiply_fusion = (f32[2,1]{1,0:T(2,128)S(1)}, f32[2,1]{1,0:T(2,128)S(1)}) fusion(f32[2,8]{1,0:T(2,128)} %cameras_ref.3), kind=kLoop, calls=%fused_computation.18 | loop fusion | flops 4 | bytes 32 | tf_op jit(solution)/shard_map/mul | solution.py:27
  1.5 1.2 %multiply_reduce_fusion.8 = (f32[2]{0:T(128)S(1)}, f32[2]{0:T(128)S(1)}, f32[2]{0:T(128)S(1)}, f32[2]{0:T(128)S(1)}, f32[2]{0:T(128)S(1)}, /*index=5*/f32[2]{0:T...) fusion(f32[2,1]{1,0:T(2,128)S(1)} %get-tuple-element.60, ...), kind=kLoop, calls=%fused_computation.8 | loop fusion | flops 46 | bytes 160 | tf_op jit(solution)/shard_map/mul | solution.py:48
  2.7 0.0 copy-start.15
  2.7 0.0 copy-start.13
  2.8 0.0 copy-start.10
  2.8 0.0 copy-start.11
  2.8 0.1 stack.2.harmonics_ref
  2.9 0.0 copy-done.3
  2.9 0.5 copy-done.15
  3.4 0.1 copy-done.13
  3.5 0.0 copy-done.10
  3.5 0.0 copy-done.11
  3.5 0.0 copy-start
  3.5 1.1 %copy-done = f32[48,4096]{1,0:T(8,128)S(1)} copy-done((f32[48,4096]{1,0:T(8,128)S(1)}, f32[48,4096]{1,0:T(8,128)}, u32[]{:S(2)}) %copy-start) | copy-done | bytes 786456
  4.6 0.0 copy-start.4
  4.6 0.8 %copy-done.4 = f32[3,4096]{1,0:T(4,128)S(1)} copy-done((f32[3,4096]{1,0:T(4,128)S(1)}, f32[3,4096]{1,0:T(4,128)}, u32[]{:S(2)}) %copy-start.4) | copy-done | bytes 49176
  5.5 0.0 copy-start.6
  5.5 0.8 %copy-done.6 = f32[3,4096]{1,0:T(4,128)S(1)} copy-done((f32[3,4096]{1,0:T(4,128)S(1)}, f32[3,4096]{1,0:T(4,128)}, u32[]{:S(2)}) %copy-start.6) | copy-done | bytes 49176
  6.3 5.8 %owner_rows.1 = (f32[16,24,128]{2,1,0:T(8,128)S(1)}, s32[64,128]{1,0:T(8,128)S(1)}, f32[8,4096]{1,0:T(8,128)S(1)}) custom-call(f32[3,4096]{1,0:T(4,128)S(1)} %copy-done.3, f32[3,4096]{1,0:T(4,128)S(1)} %copy-done.4, f32[3,4096]{1,0:T(4,128)S(1)} %copy-done.6, f32[1,4096]{1,0:T(1,128)S(1)} %bitcast.76, f32[48,4096]{1,0:T(8,128)S(1)} %copy-done, ...), custom_call_target="tpu_custom_call" | custom-call | tf_op jit(solution)/shard_map/owner_rows/pallas_call | solution.py:732
  12.2 0.0 copy-start.8
  12.2 0.7 %copy-done.8 = f32[16,24,128]{2,1,0:T(8,128)} copy-done((f32[16,24,128]{2,1,0:T(8,128)}, f32[16,24,128]{2,1,0:T(8,128)S(1)}, u32[]{:S(2)}) %copy-start.8) | copy-done | bytes 196632
  12.8 0.0 copy-start.12
  12.8 0.0 copy-start.14
  12.8 0.0 copy-start.16
  12.8 0.0 copy-start.17
  12.9 11.7 %exchange.2.pool_ref = f32[16,24,128]{2,1,0:T(8,128)} custom-call(f32[16,24,128]{2,1,0:T(8,128)} %copy-done.8), custom_call_target="tpu_custom_call" | custom-call | tf_op jit(solution)/shard_map/exchange/pallas_call | solution.py:685
  24.6 0.0 copy-done.12
  24.6 0.0 copy-done.14
  24.6 0.0 copy-done.16
  24.6 0.0 copy-done.17
  24.6 0.0 copy-start.2
  24.7 0.9 %copy-done.2 = f32[16,24,128]{2,1,0:T(8,128)S(1)} copy-done((f32[16,24,128]{2,1,0:T(8,128)S(1)}, f32[16,24,128]{2,1,0:T(8,128)}, u32[]{:S(2)}) %copy-start.2) | copy-done | bytes 196632
  25.6 23.3 %tile_blend.1 = (f32[16,24,128]{2,1,0:T(8,128)S(1)}, f32[3,8,256]{2,1,0:T(8,128)}) custom-call(f32[16,24,128]{2,1,0:T(8,128)S(1)} %copy-done.2, s32[8,512]{1,0:T(8,128)S(1)} %bitcast.80, s32[1,8]{1,0:T(1,128)S(1)} %copy-done.16, f32[1,12]{1,0:T(1,128)S(1)} %copy-done.17, f32[3,8,256]{2,1,0:T(8,128)S(1)} %bitcast.78), custom_call_target="tpu_custom_call" | custom-call | tf_op jit(solution)/shard_map/tile_blend/pallas_call | solution.py:756
  48.8 0.0 copy-start.9
  48.8 0.7 %copy-done.9 = f32[16,24,128]{2,1,0:T(8,128)} copy-done((f32[16,24,128]{2,1,0:T(8,128)}, f32[16,24,128]{2,1,0:T(8,128)S(1)}, u32[]{:S(2)}) %copy-start.9) | copy-done | bytes 196632
  49.5 0.0 copy-start.5
  49.5 0.0 copy-start.7
  49.5 9.7 %exchange.3.back_ref = f32[16,24,128]{2,1,0:T(8,128)} custom-call(f32[16,24,128]{2,1,0:T(8,128)} %copy-done.9), custom_call_target="tpu_custom_call" | custom-call | tf_op jit(solution)/shard_map/exchange/pallas_call | solution.py:685
  59.2 0.0 copy-done.5
  59.2 0.0 copy-done.7
  59.2 0.0 copy-start.1
  59.2 0.9 %copy-done.1 = f32[16,24,128]{2,1,0:T(8,128)S(1)} copy-done((f32[16,24,128]{2,1,0:T(8,128)S(1)}, f32[16,24,128]{2,1,0:T(8,128)}, u32[]{:S(2)}) %copy-start.1) | copy-done | bytes 196632
  60.1 5.7 %owner_gradient.1 = (f32[58,4096]{1,0:T(8,128)}, f32[1,12]{1,0:T(1,128)}) custom-call(f32[3,4096]{1,0:T(4,128)S(1)} %copy-done.3, f32[3,4096]{1,0:T(4,128)S(1)} %copy-done.5, f32[3,4096]{1,0:T(4,128)S(1)} %copy-done.7, f32[1,4096]{1,0:T(1,128)S(1)} %bitcast.77, f32[2,8]{1,0:T(2,128)S(1)} %copy-done.11, f32[16,2]{1,0:T(8,128)S(1)} %stack.2.harmonics_ref, ...), custom_call_target="tpu_custom_call" | custom-call | tf_op jit(solution)/shard_map/owner_gradient/pallas_call | solution.py:776
  (3 shorter events, 0.0 us)
Async XLA Ops:
  0.6 2.2 %copy-start.3 = (f32[3,4096]{1,0:T(4,128)S(1)}, f32[3,4096]{1,0:T(4,128)}, u32[]{:S(2)}) copy-start(f32[3,4096]{1,0:T(4,128)} %centers_ref.1) | copy-start | bytes 147460
  2.7 0.7 copy-start.15
  2.7 0.7 %copy-start.13 = (s32[1,16,256]{2,1,0:T(8,128)S(1)}, s32[1,16,256]{2,1,0:T(8,128)}, u32[]{:S(2)}) copy-start(s32[1,16,256]{2,1,0:T(8,128)} %param.20) | copy-start | bytes 49156
  2.8 0.7 %copy-start.10 = (f32[4096]{0:T(1024)S(1)}, f32[4096]{0:T(1024)}, u32[]{:S(2)}) copy-start(f32[4096]{0:T(1024)} %param.15) | copy-start | bytes 49156
  2.8 0.7 %copy-start.11 = (f32[2,8]{1,0:T(2,128)S(1)}, f32[2,8]{1,0:T(2,128)}, u32[]{:S(2)}) copy-start(f32[2,8]{1,0:T(2,128)} %cameras_ref.3) | copy-start | bytes 196
  3.5 1.1 %copy-start = (f32[48,4096]{1,0:T(8,128)S(1)}, f32[48,4096]{1,0:T(8,128)}, u32[]{:S(2)}) copy-start(f32[48,4096]{1,0:T(8,128)} %coeff_in.1) | copy-start | bytes 2359300
  4.6 0.8 %copy-start.4 = (f32[3,4096]{1,0:T(4,128)S(1)}, f32[3,4096]{1,0:T(4,128)}, u32[]{:S(2)}) copy-start(f32[3,4096]{1,0:T(4,128)} %scale_ref.1) | copy-start | bytes 147460
  5.5 0.8 %copy-start.6 = (f32[3,4096]{1,0:T(4,128)S(1)}, f32[3,4096]{1,0:T(4,128)}, u32[]{:S(2)}) copy-start(f32[3,4096]{1,0:T(4,128)} %shear_ref.1) | copy-start | bytes 147460
  12.2 0.7 %copy-start.8 = (f32[16,24,128]{2,1,0:T(8,128)}, f32[16,24,128]{2,1,0:T(8,128)S(1)}, u32[]{:S(2)}) copy-start(f32[16,24,128]{2,1,0:T(8,128)S(1)} %get-tuple-element.10.in_ref) | copy-start | bytes 589828
  12.8 11.8 %copy-start.12 = (f32[3,1,1,8,256]{4,3,2,1,0:T(8,128)S(1)}, f32[3,1,1,8,256]{4,3,2,1,0:T(8,128)}, u32[]{:S(2)}) copy-start(f32[3,1,1,8,256]{4,3,2,1,0:T(8,128)} %param.19) | copy-start | bytes 73732
  12.8 11.8 %copy-start.14 = (s32[1,8,512]{2,1,0:T(8,128)S(1)}, s32[1,8,512]{2,1,0:T(8,128)}, u32[]{:S(2)}) copy-start(s32[1,8,512]{2,1,0:T(8,128)} %param.22) | copy-start | bytes 49156
  12.8 11.8 %copy-start.16 = (s32[1,8]{1,0:T(1,128)S(1)}, s32[1,8]{1,0:T(1,128)}, u32[]{:S(2)}) copy-start(s32[1,8]{1,0:T(1,128)} %count_ref.3) | copy-start | bytes 100
  12.8 11.8 %copy-start.17 = (f32[1,12]{1,0:T(1,128)S(1)}, f32[1,12]{1,0:T(1,128)}, u32[]{:S(2)}) copy-start(f32[1,12]{1,0:T(1,128)} %appear_ref.1) | copy-start | bytes 148
  24.6 0.9 %copy-start.2 = (f32[16,24,128]{2,1,0:T(8,128)S(1)}, f32[16,24,128]{2,1,0:T(8,128)}, u32[]{:S(2)}) copy-start(f32[16,24,128]{2,1,0:T(8,128)} %exchange.2.pool_ref) | copy-start | bytes 589828
  48.8 0.7 %copy-start.9 = (f32[16,24,128]{2,1,0:T(8,128)}, f32[16,24,128]{2,1,0:T(8,128)S(1)}, u32[]{:S(2)}) copy-start(f32[16,24,128]{2,1,0:T(8,128)S(1)} %get-tuple-element.14.in_ref) | copy-start | bytes 589828
  49.5 9.7 %copy-start.5 = (f32[3,4096]{1,0:T(4,128)S(1)}, f32[3,4096]{1,0:T(4,128)}, u32[]{:S(2)}) copy-start(f32[3,4096]{1,0:T(4,128)} %scale_ref.1) | copy-start | bytes 147460
  49.5 9.7 %copy-start.7 = (f32[3,4096]{1,0:T(4,128)S(1)}, f32[3,4096]{1,0:T(4,128)}, u32[]{:S(2)}) copy-start(f32[3,4096]{1,0:T(4,128)} %shear_ref.1) | copy-start | bytes 147460
  59.2 0.9 %copy-start.1 = (f32[16,24,128]{2,1,0:T(8,128)S(1)}, f32[16,24,128]{2,1,0:T(8,128)}, u32[]{:S(2)}) copy-start(f32[16,24,128]{2,1,0:T(8,128)} %exchange.3.back_ref) | copy-start | bytes 589828

commit v3 on v2

--- a/solution.py
+++ b/solution.py
@@ -16,7 +16,7 @@
 NT = (((1,), (1,)), ((), ()))
 PARAMS = pltpu.CompilerParams(vmem_limit_bytes=48 * 1024 * 1024)
 IN_VMEM = pl.BlockSpec(memory_space=pltpu.VMEM)
-IN_PLACE = pl.BlockSpec(memory_space=pl.ANY)
+IN_PLACE = pl.BlockSpec(memory_space=pltpu.HBM)
 IN_SMEM = pl.BlockSpec(memory_space=pltpu.SMEM)
 
 
@@ -410,7 +410,7 @@
                     new_colors.append(colors[half * 3 + color] + weight * row[6 + color])
             return (tuple(new_transmit), tuple(new_colors))
 
-        state = lax.fori_loop(0, LANES, forward, state, unroll=32)
+        state = lax.fori_loop(0, LANES, forward, state, unroll=64)
     blended = [
         jnp.concatenate([state[1][half * 3 + color] for half in range(halves)], axis=1)
         for color in range(3)
@@ -462,7 +462,7 @@
                 alpha_ref[col * LANES + k, :, cut] = ahead * weight_ref[col * LANES + k, :, cut]
             return tuple(new_behind)
 
-        behind = lax.fori_loop(0, LANES, backward, behind, unroll=32)
+        behind = lax.fori_loop(0, LANES, backward, behind, unroll=64)
 
     pix = iota((16, tile_pix), 1)
     mono_x = (pix & 15).astype(F32) - 7.5

time: 66.3 us -> 65.1 us (0.982)
  Pallas kernels: 56.2 us -> 55 us
    pallas_call x1, Pallas kernels: 23.3 us -> 22 us  [on_device(): pl.pallas_call(functools.partial(tile_kernel, slot_cap, peers, sub_count)...]
where the time goes in v3:
time: 65.1 us; the launch traced here: 64.6 us
  Pallas kernels  55 us (84%)
  local copies, waits for them, and re-layouts  6.73 us (10%)
  other arithmetic  2.09 us (3%)
  between operations  0.81 us (1%)
    pallas_call x1, Pallas kernels, on_device(): pl.pallas_call(functools.partial(tile_kernel, slot_cap, peers, sub_count)...  22 us
    pallas_call x2, Pallas kernels, exchange(): pl.pallas_call(functools.partial(exchange_kernel, view_count, sub_count),...  21.4 us
    unnamed x36, local copies, waits for them, and re-layouts  6.67 us
    pallas_call x1, Pallas kernels, on_device(): pl.pallas_call(functools.partial(owner_kernel, sub_count, view_count, slo...  5.85 us
    pallas_call x1, Pallas kernels, on_device(): pl.pallas_call(functools.partial(gradient_kernel, sub_count, view_count,...  5.73 us

profile of v3, /device:TPU:0, one launch (start us, length us, event | category | flops | bytes accessed | tf_op | source)
XLA Modules:
  0.0 64.6 jit_solution(7343320317877773991)
XLA Ops:
  0.6 0.0 copy-start.3
  0.6 0.9 %sine_multiply_fusion = (f32[2,1]{1,0:T(2,128)S(1)}, f32[2,1]{1,0:T(2,128)S(1)}) fusion(f32[2,8]{1,0:T(2,128)} %cameras_ref.3), kind=kLoop, calls=%fused_computation.18 | loop fusion | flops 4 | bytes 32 | tf_op jit(solution)/shard_map/mul | solution.py:27
  1.5 1.2 %multiply_reduce_fusion.8 = (f32[2]{0:T(128)S(1)}, f32[2]{0:T(128)S(1)}, f32[2]{0:T(128)S(1)}, f32[2]{0:T(128)S(1)}, f32[2]{0:T(128)S(1)}, /*index=5*/f32[2]{0:T...) fusion(f32[2,1]{1,0:T(2,128)S(1)} %get-tuple-element.60, ...), kind=kLoop, calls=%fused_computation.8 | loop fusion | flops 46 | bytes 160 | tf_op jit(solution)/shard_map/mul | solution.py:48
  2.7 0.0 copy-start.15
  2.7 0.0 copy-start.13
  2.8 0.0 copy-start.10
  2.8 0.0 copy-start.11
  2.8 0.1 stack.2.harmonics_ref
  2.9 0.0 copy-done.3
  2.9 0.5 copy-done.15
  3.4 0.1 copy-done.13
  3.5 0.0 copy-done.10
  3.5 0.0 copy-done.11
  3.5 0.0 copy-start
  3.5 1.1 %copy-done = f32[48,4096]{1,0:T(8,128)S(1)} copy-done((f32[48,4096]{1,0:T(8,128)S(1)}, f32[48,4096]{1,0:T(8,128)}, u32[]{:S(2)}) %copy-start) | copy-done | bytes 786456
  4.6 0.0 copy-start.4
  4.6 0.8 %copy-done.4 = f32[3,4096]{1,0:T(4,128)S(1)} copy-done((f32[3,4096]{1,0:T(4,128)S(1)}, f32[3,4096]{1,0:T(4,128)}, u32[]{:S(2)}) %copy-start.4) | copy-done | bytes 49176
  5.5 0.0 copy-start.6
  5.5 0.8 %copy-done.6 = f32[3,4096]{1,0:T(4,128)S(1)} copy-done((f32[3,4096]{1,0:T(4,128)S(1)}, f32[3,4096]{1,0:T(4,128)}, u32[]{:S(2)}) %copy-start.6) | copy-done | bytes 49176
  6.3 5.8 %owner_rows.1 = (f32[16,24,128]{2,1,0:T(8,128)S(1)}, s32[64,128]{1,0:T(8,128)S(1)}, f32[8,4096]{1,0:T(8,128)S(1)}) custom-call(f32[3,4096]{1,0:T(4,128)S(1)} %copy-done.3, f32[3,4096]{1,0:T(4,128)S(1)} %copy-done.4, f32[3,4096]{1,0:T(4,128)S(1)} %copy-done.6, f32[1,4096]{1,0:T(1,128)S(1)} %bitcast.76, f32[48,4096]{1,0:T(8,128)S(1)} %copy-done, ...), custom_call_target="tpu_custom_call" | custom-call | tf_op jit(solution)/shard_map/owner_rows/pallas_call | solution.py:732
  12.2 0.0 copy-start.8
  12.2 0.7 %copy-done.8 = f32[16,24,128]{2,1,0:T(8,128)} copy-done((f32[16,24,128]{2,1,0:T(8,128)}, f32[16,24,128]{2,1,0:T(8,128)S(1)}, u32[]{:S(2)}) %copy-start.8) | copy-done | bytes 196632
  12.8 0.0 copy-start.12
  12.8 0.0 copy-start.14
  12.8 0.0 copy-start.16
  12.8 0.0 copy-start.17
  12.9 11.7 %exchange.2.pool_ref = f32[16,24,128]{2,1,0:T(8,128)} custom-call(f32[16,24,128]{2,1,0:T(8,128)} %copy-done.8), custom_call_target="tpu_custom_call" | custom-call | tf_op jit(solution)/shard_map/exchange/pallas_call | solution.py:685
  24.6 0.0 copy-done.12
  24.6 0.0 copy-done.14
  24.6 0.0 copy-done.16
  24.6 0.0 copy-done.17
  24.6 0.0 copy-start.2
  24.7 0.9 %copy-done.2 = f32[16,24,128]{2,1,0:T(8,128)S(1)} copy-done((f32[16,24,128]{2,1,0:T(8,128)S(1)}, f32[16,24,128]{2,1,0:T(8,128)}, u32[]{:S(2)}) %copy-start.2) | copy-done | bytes 196632
  25.6 22.0 %tile_blend.1 = (f32[16,24,128]{2,1,0:T(8,128)S(1)}, f32[3,8,256]{2,1,0:T(8,128)}) custom-call(f32[16,24,128]{2,1,0:T(8,128)S(1)} %copy-done.2, s32[8,512]{1,0:T(8,128)S(1)} %bitcast.80, s32[1,8]{1,0:T(1,128)S(1)} %copy-done.16, f32[1,12]{1,0:T(1,128)S(1)} %copy-done.17, f32[3,8,256]{2,1,0:T(8,128)S(1)} %bitcast.78), custom_call_target="tpu_custom_call" | custom-call | tf_op jit(solution)/shard_map/tile_blend/pallas_call | solution.py:756
  47.6 0.0 copy-start.9
  47.6 0.7 %copy-done.9 = f32[16,24,128]{2,1,0:T(8,128)} copy-done((f32[16,24,128]{2,1,0:T(8,128)}, f32[16,24,128]{2,1,0:T(8,128)S(1)}, u32[]{:S(2)}) %copy-start.9) | copy-done | bytes 196632
  48.3 0.0 copy-start.5
  48.3 0.0 copy-start.7
  48.3 9.7 %exchange.3.back_ref = f32[16,24,128]{2,1,0:T(8,128)} custom-call(f32[16,24,128]{2,1,0:T(8,128)} %copy-done.9), custom_call_target="tpu_custom_call" | custom-call | tf_op jit(solution)/shard_map/exchange/pallas_call | solution.py:685
  58.0 0.0 copy-done.5
  58.0 0.0 copy-done.7
  58.0 0.0 copy-start.1
  58.0 0.9 %copy-done.1 = f32[16,24,128]{2,1,0:T(8,128)S(1)} copy-done((f32[16,24,128]{2,1,0:T(8,128)S(1)}, f32[16,24,128]{2,1,0:T(8,128)}, u32[]{:S(2)}) %copy-start.1) | copy-done | bytes 196632
  58.9 5.7 %owner_gradient.1 = (f32[58,4096]{1,0:T(8,128)}, f32[1,12]{1,0:T(1,128)}) custom-call(f32[3,4096]{1,0:T(4,128)S(1)} %copy-done.3, f32[3,4096]{1,0:T(4,128)S(1)} %copy-done.5, f32[3,4096]{1,0:T(4,128)S(1)} %copy-done.7, f32[1,4096]{1,0:T(1,128)S(1)} %bitcast.77, f32[2,8]{1,0:T(2,128)S(1)} %copy-done.11, f32[16,2]{1,0:T(8,128)S(1)} %stack.2.harmonics_ref, ...), custom_call_target="tpu_custom_call" | custom-call | tf_op jit(solution)/shard_map/owner_gradient/pallas_call | solution.py:776
  (3 shorter events, 0.0 us)
Async XLA Ops:
  0.6 2.2 %copy-start.3 = (f32[3,4096]{1,0:T(4,128)S(1)}, f32[3,4096]{1,0:T(4,128)}, u32[]{:S(2)}) copy-start(f32[3,4096]{1,0:T(4,128)} %centers_ref.1) | copy-start | bytes 147460
  2.7 0.7 %copy-start.15 = (s32[1,16]{1,0:T(1,128)S(1)}, s32[1,16]{1,0:T(1,128)}, u32[]{:S(2)}) copy-start(s32[1,16]{1,0:T(1,128)} %count_ref.2) | copy-start | bytes 196
  2.7 0.7 %copy-start.13 = (s32[1,16,256]{2,1,0:T(8,128)S(1)}, s32[1,16,256]{2,1,0:T(8,128)}, u32[]{:S(2)}) copy-start(s32[1,16,256]{2,1,0:T(8,128)} %param.20) | copy-start | bytes 49156
  2.8 0.7 %copy-start.10 = (f32[4096]{0:T(1024)S(1)}, f32[4096]{0:T(1024)}, u32[]{:S(2)}) copy-start(f32[4096]{0:T(1024)} %param.15) | copy-start | bytes 49156
  2.8 0.7 %copy-start.11 = (f32[2,8]{1,0:T(2,128)S(1)}, f32[2,8]{1,0:T(2,128)}, u32[]{:S(2)}) copy-start(f32[2,8]{1,0:T(2,128)} %cameras_ref.3) | copy-start | bytes 196
  3.5 1.1 %copy-start = (f32[48,4096]{1,0:T(8,128)S(1)}, f32[48,4096]{1,0:T(8,128)}, u32[]{:S(2)}) copy-start(f32[48,4096]{1,0:T(8,128)} %coeff_in.1) | copy-start | bytes 2359300
  4.6 0.8 %copy-start.4 = (f32[3,4096]{1,0:T(4,128)S(1)}, f32[3,4096]{1,0:T(4,128)}, u32[]{:S(2)}) copy-start(f32[3,4096]{1,0:T(4,128)} %scale_ref.1) | copy-start | bytes 147460
  5.5 0.8 %copy-start.6 = (f32[3,4096]{1,0:T(4,128)S(1)}, f32[3,4096]{1,0:T(4,128)}, u32[]{:S(2)}) copy-start(f32[3,4096]{1,0:T(4,128)} %shear_ref.1) | copy-start | bytes 147460
  12.2 0.7 %copy-start.8 = (f32[16,24,128]{2,1,0:T(8,128)}, f32[16,24,128]{2,1,0:T(8,128)S(1)}, u32[]{:S(2)}) copy-start(f32[16,24,128]{2,1,0:T(8,128)S(1)} %get-tuple-element.10.in_ref) | copy-start | bytes 589828
  12.8 11.8 %copy-start.12 = (f32[3,1,1,8,256]{4,3,2,1,0:T(8,128)S(1)}, f32[3,1,1,8,256]{4,3,2,1,0:T(8,128)}, u32[]{:S(2)}) copy-start(f32[3,1,1,8,256]{4,3,2,1,0:T(8,128)} %param.19) | copy-start | bytes 73732
  12.8 11.8 %copy-start.14 = (s32[1,8,512]{2,1,0:T(8,128)S(1)}, s32[1,8,512]{2,1,0:T(8,128)}, u32[]{:S(2)}) copy-start(s32[1,8,512]{2,1,0:T(8,128)} %param.22) | copy-start | bytes 49156
  12.8 11.8 %copy-start.16 = (s32[1,8]{1,0:T(1,128)S(1)}, s32[1,8]{1,0:T(1,128)}, u32[]{:S(2)}) copy-start(s32[1,8]{1,0:T(1,128)} %count_ref.3) | copy-start | bytes 100
  12.8 11.8 %copy-start.17 = (f32[1,12]{1,0:T(1,128)S(1)}, f32[1,12]{1,0:T(1,128)}, u32[]{:S(2)}) copy-start(f32[1,12]{1,0:T(1,128)} %appear_ref.1) | copy-start | bytes 148
  24.6 0.9 %copy-start.2 = (f32[16,24,128]{2,1,0:T(8,128)S(1)}, f32[16,24,128]{2,1,0:T(8,128)}, u32[]{:S(2)}) copy-start(f32[16,24,128]{2,1,0:T(8,128)} %exchange.2.pool_ref) | copy-start | bytes 589828
  47.6 0.7 %copy-start.9 = (f32[16,24,128]{2,1,0:T(8,128)}, f32[16,24,128]{2,1,0:T(8,128)S(1)}, u32[]{:S(2)}) copy-start(f32[16,24,128]{2,1,0:T(8,128)S(1)} %get-tuple-element.14.in_ref) | copy-start | bytes 589828
  48.3 9.7 %copy-start.5 = (f32[3,4096]{1,0:T(4,128)S(1)}, f32[3,4096]{1,0:T(4,128)}, u32[]{:S(2)}) copy-start(f32[3,4096]{1,0:T(4,128)} %scale_ref.1) | copy-start | bytes 147460
  48.3 9.7 %copy-start.7 = (f32[3,4096]{1,0:T(4,128)S(1)}, f32[3,4096]{1,0:T(4,128)}, u32[]{:S(2)}) copy-start(f32[3,4096]{1,0:T(4,128)} %shear_ref.1) | copy-start | bytes 147460
  58.0 0.9 %copy-start.1 = (f32[16,24,128]{2,1,0:T(8,128)S(1)}, f32[16,24,128]{2,1,0:T(8,128)}, u32[]{:S(2)}) copy-start(f32[16,24,128]{2,1,0:T(8,128)} %exchange.3.back_ref) | copy-start | bytes 589828
